TPU v7x, 256 devices: a whole 4x4x8 slice. The times are simulated.
256 devices in a mesh: src: 128 (over x, z, y), tgt: 2 (over core).
Axes of the slice: x: 4, y: 4, z: 8, core: 2. Of those that a mesh axis runs over, the one named last changes fastest.
Arguments:
- x_src: bfloat16 [64, 524288], P(None, 'src'), may hold values from -6 to 6
- w_src: float32 [524288], P('src'), may hold values from 13 to 310
- y_tgt: bfloat16 [64, 2097152], P(None, 'src'), may hold values from -6 to 6
- g_in: bfloat16 [2097152], P('src'), may hold values from 0 to 31
- support_owner: int32 [2, 2048, 8], P('tgt', 'src'), may hold values from 0 to 127, all different within a row; in each aligned block of 16 rows (0 to 15, 16 to 31, ..., all dimensions but the last counted through in order) at most 2 rows name the same one
- support_local: int32 [2, 2048, 8], P('tgt', 'src'), may hold values from 0 to 31
- live_count: int32 [2, 2048], P('tgt', 'src'), may hold values from 5 to 8
Outputs:
- f_new: float32 [524288], P('src')
- g_new: float32 [2097152], P('src')
Inputs may be any that keep to these rules, and one draw needn't show every extreme that they name: `support_owner`: in each list half the 8 owners named by one row block are distinct, and the 16 row blocks of one device name one owner in at most 2 slots of that half.
All inputs are finite; a program needn't handle non-finite values.
Results may differ from a plain program's by a relative error of at most 0.0003.
Values may be sent and summed in bfloat16 or wider, within the bound.
A program may use at most 64 MiB of HBM per device.

v0:
```python
import math

import jax
import jax.numpy as jnp
from jax import lax
from jax.sharding import PartitionSpec as P

DIM = 64
BLK = 256
KH = 8
RB_DEV = 16
TB_DEV = 64


EPSILON = 0.1
EMPTY = -1e30


def joined(array, axis, combine):
    everything = jax.tree.map(lambda part: lax.all_gather(part, axis), array)
    initial = jax.tree.map(lambda part: part[0], everything)

    def lap(k, so_far):
        return combine(so_far, jax.tree.map(lambda part: part[k], everything))

    return lax.fori_loop(1, lax.axis_size(axis), lap, initial)


def pair_merge(earlier, latter):
    peak_value = jnp.maximum(earlier[0], latter[0])
    return (
        peak_value,
        earlier[1] * jnp.exp(earlier[0] - peak_value) + latter[1] * jnp.exp(latter[0] - peak_value),
    )


def potential(peak_value, mass_sum):
    ceiling = jnp.maximum(peak_value, 0.0)
    return -EPSILON * (
        ceiling + jnp.log(jnp.exp(-ceiling) + mass_sum * jnp.exp(peak_value - ceiling))
    )


def squares(tile_data):
    return jnp.sum(jnp.square(tile_data.astype(jnp.float32)), axis=-2)


def paired_costs(row_tiles, row_squares, col_tiles, col_squares):
    cross_terms = jnp.einsum(
        "ldc,lde->lce", row_tiles, col_tiles, preferred_element_type=jnp.float32
    )
    return (row_squares[:, :, None] + col_squares[:, None, :] - 2.0 * cross_terms) / DIM


def row_part(tile_cost, potentials, alive_mask):
    logits = (potentials[:, None, :] - tile_cost) / EPSILON
    peak_value = jnp.max(logits, axis=2)
    mass_sum = jnp.sum(jnp.exp(logits - peak_value[:, :, None]), axis=2)
    return (
        jnp.where(alive_mask[:, None], peak_value, EMPTY),
        jnp.where(alive_mask[:, None], mass_sum, 0.0),
    )


def column_part(tile_cost, potentials, log_weights, alive_mask):
    logits = (potentials[:, :, None] - tile_cost) / EPSILON + log_weights[:, :, None]
    peak_value = jnp.max(logits, axis=1)
    mass_sum = jnp.sum(jnp.exp(logits - peak_value[:, None, :]), axis=1)
    return (
        jnp.where(alive_mask[:, None], peak_value, EMPTY),
        jnp.where(alive_mask[:, None], mass_sum, 0.0),
    )


def grouped(function, arrays):
    total_rows = arrays[0].shape[0]
    group_size = math.gcd(total_rows, 16)
    shaped = tuple(
        (
            member.reshape((total_rows // group_size, group_size) + member.shape[1:])
            for member in arrays
        )
    )
    results = lax.map(function, shaped)
    return tuple((result.reshape((total_rows,) + result.shape[2:]) for result in results))


def row_finish(slot_peaks, slot_sums):
    peak_grid = slot_peaks.reshape(RB_DEV, KH, BLK)
    sum_grid = slot_sums.reshape(RB_DEV, KH, BLK)
    block_peak = jnp.max(peak_grid, axis=1)
    block_sum = jnp.sum(sum_grid * jnp.exp(peak_grid - block_peak[:, None, :]), axis=1)
    merged = joined((block_peak, block_sum), "tgt", pair_merge)
    return potential(merged[0], merged[1])


def close_columns(owner_ids, col_peaks, col_sums, core_half):
    target_index = jnp.where(owner_ids >= 0, owner_ids, TB_DEV)
    col_peak = (
        jnp.full((TB_DEV, BLK), EMPTY, jnp.float32).at[target_index].max(col_peaks, mode="drop")
    )
    lookup = col_peak[jnp.minimum(target_index, TB_DEV - 1)]
    col_total = (
        jnp.zeros((TB_DEV, BLK), jnp.float32)
        .at[target_index]
        .add(col_sums * jnp.exp(col_peaks - lookup), mode="drop")
    )
    half_width = TB_DEV // 2
    own_half = lax.dynamic_slice_in_dim(
        potential(col_peak, col_total), core_half * half_width, half_width, 0
    )
    return own_half.reshape(half_width * BLK)


def on_device(x_src, w_src, y_tgt, g_in, support_owner, support_local, live_count):
    peer_count = lax.axis_size("src")
    core_half = lax.axis_index("tgt")
    capacity = min(RB_DEV, max(2, (2 * RB_DEV * KH + peer_count - 1) // peer_count))
    slot_count = RB_DEV * KH
    buffer_count = peer_count * capacity
    owners = support_owner[0].reshape(slot_count)
    local_ids = core_half * (TB_DEV // 2) + support_local[0].reshape(slot_count)
    alive_slots = (
        lax.broadcasted_iota(jnp.int32, (RB_DEV, KH), 1) < live_count[0][:, None]
    ).reshape(slot_count)
    slot_order = lax.iota(jnp.int32, slot_count)
    earlier_same = (
        (owners[:, None] == owners[None, :])
        & alive_slots[None, :]
        & (slot_order[None, :] < slot_order[:, None])
    )
    position = jnp.sum(earlier_same.astype(jnp.int32), axis=1)
    buffer_slot = owners * capacity + position
    matches = (buffer_slot[:, None] == lax.iota(jnp.int32, buffer_count)[None, :]) & alive_slots[
        :, None
    ]
    row_of = jnp.sum(jnp.where(matches, (slot_order // KH)[:, None], 0), axis=0)
    asked_ids = jnp.sum(jnp.where(matches, local_ids[:, None] + 1, 0), axis=0) - 1
    read_at = jnp.where(alive_slots, buffer_slot, 0)
    source_rows = x_src.reshape(DIM, RB_DEV, BLK).transpose(1, 0, 2)
    target_rows = y_tgt.reshape(DIM, TB_DEV, BLK).transpose(1, 0, 2)
    target_squares = squares(target_rows)
    target_pots = g_in.reshape(TB_DEV, BLK)
    weight_rows = w_src.reshape(RB_DEV, BLK)
    outgoing = jnp.take(source_rows, row_of, axis=0).reshape(peer_count, capacity, DIM, BLK)
    outgoing_ids = asked_ids.astype(jnp.bfloat16).reshape(peer_count, capacity)
    tile_data = lax.all_to_all(outgoing, "src", split_axis=0, concat_axis=0, tiled=True)
    block_code = lax.all_to_all(outgoing_ids, "src", split_axis=0, concat_axis=0, tiled=True)
    item_count = block_code.shape[1]
    block_ids = block_code.astype(jnp.int32).reshape(peer_count * item_count)
    flat_tiles = tile_data.reshape(peer_count * item_count, DIM, BLK)

    def per_group(members):
        row_tiles, member_ids = members
        chosen = jnp.clip(member_ids, 0, TB_DEV - 1)
        tile_cost = paired_costs(
            row_tiles,
            squares(row_tiles),
            jnp.take(target_rows, chosen, axis=0),
            jnp.take(target_squares, chosen, axis=0),
        )
        return row_part(
            tile_cost, jnp.take(target_pots, chosen, axis=0).astype(jnp.float32), member_ids >= 0
        )

    peak_flat, sum_flat = grouped(per_group, (flat_tiles, block_ids))
    row_peaks = lax.all_to_all(
        peak_flat.reshape(peer_count, item_count, BLK),
        "src",
        split_axis=0,
        concat_axis=0,
        tiled=True,
    )
    row_sums = lax.all_to_all(
        sum_flat.reshape(peer_count, item_count, BLK),
        "src",
        split_axis=0,
        concat_axis=0,
        tiled=True,
    )
    kept_ids = block_ids.reshape(peer_count, item_count)
    slot_peaks = jnp.where(
        alive_slots[:, None], jnp.take(row_peaks.reshape(buffer_count, BLK), read_at, axis=0), EMPTY
    )
    slot_sums = jnp.where(
        alive_slots[:, None], jnp.take(row_sums.reshape(buffer_count, BLK), read_at, axis=0), 0.0
    )
    new_source = row_finish(slot_peaks, slot_sums)
    sent_pots = jnp.take(new_source, row_of, axis=0).reshape(peer_count, capacity, BLK)
    sent_weights = jnp.take(weight_rows, row_of, axis=0).reshape(peer_count, capacity, BLK)
    got_pots, got_weights = (
        lax.all_to_all(sent_pots, "src", split_axis=0, concat_axis=0, tiled=True),
        lax.all_to_all(sent_weights, "src", split_axis=0, concat_axis=0, tiled=True),
    )
    owner_ids = kept_ids.reshape(buffer_count)

    def per_column_group(members):
        row_tiles, member_ids, pots_in, weights_in = members
        chosen = jnp.clip(member_ids, 0, TB_DEV - 1)
        tile_cost = paired_costs(
            row_tiles,
            squares(row_tiles),
            jnp.take(target_rows, chosen, axis=0),
            jnp.take(target_squares, chosen, axis=0),
        )
        return column_part(tile_cost, pots_in, weights_in, member_ids >= 0)

    col_peaks, col_sums = grouped(
        per_column_group,
        (
            tile_data.reshape(buffer_count, DIM, BLK),
            owner_ids,
            got_pots.reshape(buffer_count, BLK),
            got_weights.reshape(buffer_count, BLK),
        ),
    )
    own_half = close_columns(owner_ids, col_peaks, col_sums, core_half)
    new_target = lax.all_gather(own_half, "tgt", axis=0, tiled=True)
    return (new_source.reshape(RB_DEV * BLK), new_target)


def solution(mesh):
    placed = (
        P(None, "src"),
        P("src"),
        P(None, "src"),
        P("src"),
        P("tgt", "src", None),
        P("tgt", "src", None),
        P("tgt", "src"),
    )
    return jax.shard_map(
        on_device, mesh=mesh, in_specs=placed, out_specs=(P("src"), P("src")), check_vma=False
    )
```

profile of v0, /device:TPU:1, one launch (start us, length us, event | category | flops | bytes accessed | tf_op | source)
XLA Modules:
  0.0 631.9 jit_solution(437043704189798194)
XLA Ops:
  4.4 16.3 %all-to-all-start = ((bf16[128,1,2]{2,1,0:T(2,128)(2,1)}), bf16[128,1,2]{2,1,0:T(2,128)(2,1)S(1)}, u32[]{:S(2)}, u32[]{:S(2)}) async-start(bf16[128,1,2]{2,1,0:T(2,128)(2,1)} %convert_element_type.67), calls=%async_computation | async-start | bytes 131072 | tf_op jit(solution)/shard_map/all_to_all | solution.py:148
  22.0 9.2 %all-to-all-done = bf16[128,1,2]{2,1,0:T(2,128)(2,1)S(1)} async-done(((bf16[128,1,2]{2,1,0:T(2,128)(2,1)}), bf16[128,1,2]{2,1,0:T(2,128)(2,1)S(1)}, u32[]{:S(2)}, u32[]{:S(2)}) %all-to-all-start) | async-done | bytes 544 | tf_op jit(solution)/shard_map/all_to_all | solution.py:148
  31.4 8.4 %gather_fusion.5 = bf16[256,64,256]{2,1,0:T(8,128)(2,1)} fusion(bf16[16,64,256]{2,1,0:T(8,128)(2,1)S(1)} %bitcast.119, s32[1024]{0:T(1024)S(1)} %pad_clamp_fusion.6), kind=kCustom, calls=%fused_computation.9 | custom fusion | bytes 16778240 | tf_op jit(solution)/shard_map/jit(_take)/gather | solution.py:145
  39.8 7.4 %broadcast_select_fusion.2 = bf16[128,2,64,256]{3,2,1,0:T(8,128)(2,1)} fusion(bf16[128,2,64,256]{3,2,1,0:T(8,128)(2,1)} %bitcast.120, pred[128,2]{1,0:T(8,128)(4,1)S(1)} %compare_and_fusion.2), kind=kLoop, calls=%fused_computation.63 | loop fusion | flops 4194304 | bytes 16777472 | tf_op jit(solution)/shard_map/jit(_take)/select_n | solution.py:145
  47.3 7.8 %all-to-all-start.1 = ((bf16[128,2,64,256]{3,2,1,0:T(8,128)(2,1)}), bf16[128,2,64,256]{3,2,1,0:T(8,128)(2,1)}, u32[]{:S(2)}, u32[]{:S(2)}) async-start(bf16[128,2,64,256]{3,2,1,0:T(8,128)(2,1)} %broadcast_select_fusion.2), calls=%async_computation.1 | async-start | bytes 16777216 | tf_op jit(solution)/shard_map/all_to_all | solution.py:147
  60.5 177.8 %all-to-all-done.1 = bf16[128,2,64,256]{3,2,1,0:T(8,128)(2,1)} async-done(((bf16[128,2,64,256]{3,2,1,0:T(8,128)(2,1)}), bf16[128,2,64,256]{3,2,1,0:T(8,128)(2,1)}, u32[]{:S(2)}, u32[]{:S(2)}) %all-to-all-start.1) | async-done | bytes 8388640 | tf_op jit(solution)/shard_map/all_to_all | solution.py:147
  238.4 144.3 %while.8 = (s32[]{:T(128)}, f32[16,16,256]{2,1,0:T(8,128)S(1)}, f32[16,16,256]{2,1,0:T(8,128)S(1)}, s32[16,16]{1,0:T(8,128)S(1)}, bf16[64,256]{1,0:T(8,128)(2,1)...) while((s32[]{:T(128)}, f32[16,16,256]{2,1,0:T(8,128)S(1)}, ...), condition=%wide.region_8.11_spmd, body=%wide.region_4.0_spmd.sunk | while | flops 151005376 | bytes 11355969 | solution.py:84
  383.6 9.0 %all-to-all-start.2 = ((f32[128,2,256]{2,1,0:T(2,128)}), f32[128,2,256]{2,1,0:T(2,128)S(1)}, u32[]{:S(2)}, u32[]{:S(2)}) async-start(f32[128,2,256]{2,1,0:T(2,128)} %reshape_reshape.18), calls=%async_computation.2 | async-start | bytes 524288 | tf_op jit(solution)/shard_map/all_to_all | solution.py:167
  393.4 11.1 %all-to-all-done.2 = f32[128,2,256]{2,1,0:T(2,128)S(1)} async-done(((f32[128,2,256]{2,1,0:T(2,128)}), f32[128,2,256]{2,1,0:T(2,128)S(1)}, u32[]{:S(2)}, u32[]{:S(2)}) %all-to-all-start.2) | async-done | bytes 262176 | tf_op jit(solution)/shard_map/all_to_all | solution.py:167
  404.5 6.3 %all-to-all-start.3 = ((f32[128,2,256]{2,1,0:T(2,128)}), f32[128,2,256]{2,1,0:T(2,128)S(1)}, u32[]{:S(2)}, u32[]{:S(2)}) async-start(f32[128,2,256]{2,1,0:T(2,128)} %reshape_reshape.19), calls=%async_computation.3 | async-start | bytes 524288 | tf_op jit(solution)/shard_map/all_to_all | solution.py:174
  412.9 9.9 %all-to-all-done.3 = f32[128,2,256]{2,1,0:T(2,128)S(1)} async-done(((f32[128,2,256]{2,1,0:T(2,128)}), f32[128,2,256]{2,1,0:T(2,128)S(1)}, u32[]{:S(2)}, u32[]{:S(2)}) %all-to-all-start.3) | async-done | bytes 262176 | tf_op jit(solution)/shard_map/all_to_all | solution.py:174
  423.9 6.3 %all-gather = f32[32,256]{1,0:T(8,128)S(1)} all-gather(f32[16,256]{1,0:T(8,128)S(1)} %bitcast_reduce_fusion), channel_id=2, replica_groups=mesh['src'=128,'tgt'=2] {'tgt'}, dimensions={0}, use_global_device_ids=true | all-gather | bytes 49152 | tf_op jit(solution)/shard_map/all_gather | solution.py:20
  434.2 6.4 %all-to-all-start.4 = ((f32[128,2,256]{2,1,0:T(2,128)}), f32[128,2,256]{2,1,0:T(2,128)S(1)}, u32[]{:S(2)}, u32[]{:S(2)}) async-start(f32[128,2,256]{2,1,0:T(2,128)} %reshape.405), calls=%async_computation.4 | async-start | bytes 524288 | tf_op jit(solution)/shard_map/all_to_all | solution.py:192
  441.4 12.5 %all-to-all-done.4 = f32[128,2,256]{2,1,0:T(2,128)S(1)} async-done(((f32[128,2,256]{2,1,0:T(2,128)}), f32[128,2,256]{2,1,0:T(2,128)S(1)}, u32[]{:S(2)}, u32[]{:S(2)}) %all-to-all-start.4) | async-done | bytes 262176 | tf_op jit(solution)/shard_map/all_to_all | solution.py:192
  453.9 6.6 %all-to-all-start.5 = ((f32[128,2,256]{2,1,0:T(2,128)}), f32[128,2,256]{2,1,0:T(2,128)S(1)}, u32[]{:S(2)}, u32[]{:S(2)}) async-start(f32[128,2,256]{2,1,0:T(2,128)} %reshape.407), calls=%async_computation.5 | async-start | bytes 524288 | tf_op jit(solution)/shard_map/all_to_all | solution.py:193
  461.5 11.0 %all-to-all-done.5 = f32[128,2,256]{2,1,0:T(2,128)S(1)} async-done(((f32[128,2,256]{2,1,0:T(2,128)}), f32[128,2,256]{2,1,0:T(2,128)S(1)}, u32[]{:S(2)}, u32[]{:S(2)}) %all-to-all-start.5) | async-done | bytes 262176 | tf_op jit(solution)/shard_map/all_to_all | solution.py:193
  473.4 147.7 %while.9 = (s32[]{:T(128)}, f32[16,16,256]{2,1,0:T(8,128)S(1)}, f32[16,16,256]{2,1,0:T(8,128)S(1)}, s32[16,16]{1,0:T(8,128)S(1)}, f32[16,16,256]{2,1,0:T(8,128)S...) while((s32[]{:T(128)}, f32[16,16,256]{2,1,0:T(8,128)S(1)}, ...), condition=%wide.region_15.20_spmd, body=%wide.region_11.19_spmd.sunk | while | flops 153093248 | bytes 11408953 | solution.py:84
  476.6 3.9 fusion.61
  485.9 3.9 fusion.61
  495.1 3.9 fusion.61
  504.3 3.9 fusion.61
  513.5 3.9 fusion.61
  522.8 3.9 fusion.61
  532.0 3.9 fusion.61
  541.2 3.9 fusion.61
  550.5 3.9 fusion.61
  559.7 3.9 fusion.61
  578.2 3.9 fusion.61
  587.4 3.9 fusion.61
  596.6 3.9 fusion.61
  615.1 3.9 fusion.61
  626.2 5.1 all_gather.19
  (460 shorter events, 263.2 us)
Async XLA Ops:
  4.4 26.8 %all-to-all-start = ((bf16[128,1,2]{2,1,0:T(2,128)(2,1)}), bf16[128,1,2]{2,1,0:T(2,128)(2,1)S(1)}, u32[]{:S(2)}, u32[]{:S(2)}) async-start(bf16[128,1,2]{2,1,0:T(2,128)(2,1)} %convert_element_type.67), calls=%async_computation | async-start | bytes 131072 | tf_op jit(solution)/shard_map/all_to_all | solution.py:148
  47.3 7.8 %copy-start.1 = (bf16[64,16384]{1,0:T(8,128)(2,1)S(1)}, bf16[64,16384]{1,0:T(8,128)(2,1)}, u32[]{:S(2)}) copy-start(bf16[64,16384]{1,0:T(8,128)(2,1)} %param.21) | copy-start | bytes 6291460
  47.3 191.1 %all-to-all-start.1 = ((bf16[128,2,64,256]{3,2,1,0:T(8,128)(2,1)}), bf16[128,2,64,256]{3,2,1,0:T(8,128)(2,1)}, u32[]{:S(2)}, u32[]{:S(2)}) async-start(bf16[128,2,64,256]{3,2,1,0:T(8,128)(2,1)} %broadcast_select_fusion.2), calls=%async_computation.1 | async-start | bytes 16777216 | tf_op jit(solution)/shard_map/all_to_all | solution.py:147
  55.1 3.1 copy-start.2
  55.6 1.4 copy-start
  238.4 172.4 %copy-start.3 = (f32[4096]{0:T(1024)S(1)}, f32[4096]{0:T(1024)}, u32[]{:S(2)}) copy-start(f32[4096]{0:T(1024)} %param.20) | copy-start | bytes 49156
  383.6 20.9 %all-to-all-start.2 = ((f32[128,2,256]{2,1,0:T(2,128)}), f32[128,2,256]{2,1,0:T(2,128)S(1)}, u32[]{:S(2)}, u32[]{:S(2)}) async-start(f32[128,2,256]{2,1,0:T(2,128)} %reshape_reshape.18), calls=%async_computation.2 | async-start | bytes 524288 | tf_op jit(solution)/shard_map/all_to_all | solution.py:167
  404.5 18.3 %all-to-all-start.3 = ((f32[128,2,256]{2,1,0:T(2,128)}), f32[128,2,256]{2,1,0:T(2,128)S(1)}, u32[]{:S(2)}, u32[]{:S(2)}) async-start(f32[128,2,256]{2,1,0:T(2,128)} %reshape_reshape.19), calls=%async_computation.3 | async-start | bytes 524288 | tf_op jit(solution)/shard_map/all_to_all | solution.py:174
  434.2 19.8 %all-to-all-start.4 = ((f32[128,2,256]{2,1,0:T(2,128)}), f32[128,2,256]{2,1,0:T(2,128)S(1)}, u32[]{:S(2)}, u32[]{:S(2)}) async-start(f32[128,2,256]{2,1,0:T(2,128)} %reshape.405), calls=%async_computation.4 | async-start | bytes 524288 | tf_op jit(solution)/shard_map/all_to_all | solution.py:192
  453.9 18.6 %all-to-all-start.5 = ((f32[128,2,256]{2,1,0:T(2,128)}), f32[128,2,256]{2,1,0:T(2,128)S(1)}, u32[]{:S(2)}, u32[]{:S(2)}) async-start(f32[128,2,256]{2,1,0:T(2,128)} %reshape.407), calls=%async_computation.5 | async-start | bytes 524288 | tf_op jit(solution)/shard_map/all_to_all | solution.py:193
where the time goes:
time: 637 us; the launch traced here: 632 us
  waiting for transfers between devices  232 us (36%)
  other arithmetic  129 us (20%)
  matrix products  120 us (19%)
  local copies, waits for them, and re-layouts  83 us (13%)
  starting transfers between devices  52.5 us (8%)
  blocking collectives  13.3 us (2%)
    all_to_all x1, waiting for transfers between devices, on_device(): lax.all_to_all(outgoing, 'src', split_axis=0, concat_axis=0, tiled=True)  178 us
    dot_general x32, matrix products, paired_costs(): jnp.einsum('ldc,lde->lce', row_tiles, col_tiles, preferred_element_type=j...  120 us
    reduce_sum x33, other arithmetic, squares(): return jnp.sum(jnp.square(tile_data.astype(jnp.float32)), axis=-2)  39.7 us
    reduce_sum x16, other arithmetic, row_part(): mass_sum = jnp.sum(jnp.exp(logits - peak_value[:, :, None]), axis=2)  34.6 us
    reduce_sum x16, other arithmetic, column_part(): mass_sum = jnp.sum(jnp.exp(logits - peak_value[:, None, :]), axis=1)  32.7 us
    all_to_all x1, starting transfers between devices, on_device(): lax.all_to_all(outgoing_ids, 'src', split_axis=0, concat_axis=0, tiled=True)  16.3 us
  transfers between devices with their start and end apart: 6, of which 6 were waited for; matrix products, arithmetic and copies ran while one was open for 2% of the time, Pallas kernels for 0%

commit v1 on v0

v1 whole, which is shorter than its diff:
```python
import jax
import jax.numpy as jnp
import numpy as np
from jax import lax
from jax.experimental import pallas as pl
from jax.experimental.pallas import tpu as pltpu
from jax.sharding import Mesh, PartitionSpec as P

DIM = 64
BLK = 256
KH = 8
RB_DEV = 16
TB_DEV = 64
HALF = TB_DEV // 2

EPSILON = 0.1
EMPTY = -1e30
PER = 2.0 / (DIM * EPSILON)
PER2 = PER * float(np.log2(np.e))
OFFSET = DIM / 2.0
LN2 = float(np.log(2.0))
AUG = 16
UNROLL = 2


def split3(row):
    high = row.astype(jnp.bfloat16).astype(jnp.float32)
    middle = (row - high).astype(jnp.bfloat16).astype(jnp.float32)
    low = row - high - middle
    at = lax.broadcasted_iota(jnp.int32, (AUG, BLK), 0)
    rows = jnp.where(at == 0, high, jnp.where(at == 1, middle, jnp.where(at == 2, low, 0.0)))
    return rows.astype(jnp.bfloat16)


def three_ones():
    at = lax.broadcasted_iota(jnp.int32, (AUG, BLK), 0)
    return jnp.where(at < 3, 1.0, 0.0).astype(jnp.bfloat16)


def tile_logits(left, right):
    return lax.dot_general(
        left, right, (((0,), (0,)), ((), ())), preferred_element_type=jnp.float32
    )


def peak_and_mass(tile):
    peak = jnp.max(tile, axis=0, keepdims=True)
    mass = jnp.sum(jnp.exp2((tile - peak) * PER2), axis=0, keepdims=True)
    return peak, mass


def lane_block(index):
    return pl.ds(pl.multiple_of(index * BLK, BLK), BLK)


def x_tile(x_ref, block):
    return x_ref[block // KH, :, lane_block(block % KH)]


def y_tile(y_ref, block):
    return y_ref[block // HALF, :, lane_block(block % HALF)]


def row_kernel(items_ref, count_ref, x_ref, y_ref, bias_ref, out_ref, slots):
    slots[...] = jnp.full(slots.shape, EMPTY, jnp.float32)
    ones = three_ones()

    def step(group, carry):
        for k in range(UNROLL):
            code = items_ref[group * UNROLL + k]
            row, col = code // 256, code % 256
            safe = col % 128
            left = jnp.concatenate(
                [y_tile(y_ref, safe), split3(bias_ref[pl.ds(safe, 1), :])], axis=0
            )
            right = jnp.concatenate([x_tile(x_ref, row), ones], axis=0)
            peak, mass = peak_and_mass(tile_logits(left, right))
            slots[col // HALF, pl.ds(row, 1), :] = peak * PER2 + jnp.log2(mass)
        return carry

    lax.fori_loop(0, (count_ref[0] + UNROLL - 1) // UNROLL, step, 0)
    parts = [slots[k] for k in range(4)]
    top = jnp.maximum(jnp.maximum(parts[0], parts[1]), jnp.maximum(parts[2], parts[3]))
    total = sum(jnp.exp2(part - top) for part in parts)
    out_ref[...] = top + jnp.log2(total)


def column_kernel(items_ref, count_ref, x_ref, y_ref, bias_ref, out_ref, peaks, masses):
    peaks[...] = jnp.full(peaks.shape, EMPTY, jnp.float32)
    masses[...] = jnp.zeros(masses.shape, jnp.float32)
    ones = three_ones()

    def step(group, carry):
        for k in range(UNROLL):
            code = items_ref[group * UNROLL + k]
            row, col = code // 256, code % 256
            left = jnp.concatenate(
                [x_tile(x_ref, row), split3(bias_ref[pl.ds(row, 1), :])], axis=0
            )
            right = jnp.concatenate([y_tile(y_ref, col % 128), ones], axis=0)
            peak, mass = peak_and_mass(tile_logits(left, right))
            old = peaks[pl.ds(col, 1), :]
            new = jnp.maximum(old, peak)
            peaks[pl.ds(col, 1), :] = new
            masses[pl.ds(col, 1), :] = masses[pl.ds(col, 1), :] * jnp.exp2(
                (old - new) * PER2
            ) + mass * jnp.exp2((peak - new) * PER2)
        return carry

    lax.fori_loop(0, (count_ref[0] + UNROLL - 1) // UNROLL, step, 0)
    mass = masses[0:128, :]
    out_ref[...] = jnp.where(mass > 0.0, peaks[0:128, :] * PER2 + jnp.log2(mass), EMPTY)


SMEM = pl.BlockSpec(memory_space=pltpu.SMEM)
VMEM = pl.BlockSpec(memory_space=pltpu.VMEM)


def local_call(body, out_rows, scratch, name):
    return pl.pallas_call(
        body,
        out_shape=jax.ShapeDtypeStruct((out_rows, BLK), jnp.float32),
        in_specs=[SMEM, SMEM, VMEM, VMEM, VMEM],
        out_specs=VMEM,
        scratch_shapes=scratch,
        compiler_params=pltpu.CompilerParams(vmem_limit_bytes=48 * 1024 * 1024),
        name=name,
    )


def half_squares(tile):
    return 0.5 * jnp.sum(jnp.square(tile.astype(jnp.float32)), axis=0)


def potential(logit2):
    logit = logit2 * LN2
    top = jnp.maximum(logit, 0.0)
    return -EPSILON * (top + jnp.log(jnp.exp(-top) + jnp.exp(logit - top)))


def merged(parts):
    top = jnp.max(parts, axis=0)
    return top + jnp.log2(jnp.sum(jnp.exp2(parts - top[None]), axis=0))


def on_device(x_src, w_src, y_tgt, g_in, support_owner, support_local, live_count):
    core = lax.axis_index("core")
    here = lax.axis_index("z") * lax.axis_size("y") + lax.axis_index("y")
    plane = ("z", "y", "core")
    lines = lax.axis_size("z") * lax.axis_size("y")
    rows = lines * RB_DEV
    half_rows = RB_DEV // 2

    x_half = lax.dynamic_slice_in_dim(x_src, core * half_rows * BLK, half_rows * BLK, 1)
    w_half = lax.dynamic_slice_in_dim(w_src, core * half_rows * BLK, half_rows * BLK, 0)
    y_half = lax.dynamic_slice_in_dim(y_tgt, core * HALF * BLK, HALF * BLK, 1)
    g_half = lax.dynamic_slice_in_dim(g_in, core * HALF * BLK, HALF * BLK, 0)
    x_squares = half_squares(x_half)
    y_squares = half_squares(y_half)
    y_bias = OFFSET * g_half.astype(jnp.float32) - y_squares

    live = lax.broadcasted_iota(jnp.int32, (RB_DEV, KH), 1) < live_count[0][:, None]
    listed = jnp.where(live, support_owner[0] * HALF + support_local[0], -1)
    listed = lax.all_gather(listed.T, ("z", "y"), axis=1, tiled=True)
    x_all = lax.all_gather(x_half, plane)
    y_all = lax.all_gather(y_half, "x")
    bias_all = lax.all_gather(y_bias.reshape(HALF, BLK), "x", tiled=True)

    owner = listed // HALF
    match = (listed >= 0) & (owner % lines == here)
    codes = (
        lax.broadcasted_iota(jnp.int32, (KH, rows), 1) * 256
        + (owner // lines) * HALF
        + listed % HALF
    )
    hits = match.astype(jnp.int32)
    per_row = jnp.sum(hits, axis=0)
    order = lax.iota(jnp.int32, rows)
    before = jnp.sum(jnp.where(order[:, None] < order[None, :], per_row[:, None], 0), axis=0)
    earlier = jnp.concatenate(
        [jnp.sum(hits[:k], axis=0, keepdims=True) for k in range(KH)], axis=0
    )
    place = jnp.where(match, before[None, :] + earlier, -1)
    most = 256
    spot = lax.iota(jnp.int32, most)
    items = jnp.sum(
        jnp.where(spot[:, None, None] == place[None], codes[None], 0), axis=(1, 2)
    )
    count = jnp.sum(per_row)
    items = jnp.where(spot < count, items, 128)
    count = count.reshape(1)

    partial = local_call(
        row_kernel, rows, [pltpu.VMEM((5, rows, BLK), jnp.float32)], "rows"
    )(items, count, x_all, y_all, bias_all)
    partial = lax.all_to_all(
        partial.reshape(2 * lines, half_rows, BLK), plane, split_axis=0, concat_axis=0, tiled=True
    )
    squares = x_squares.reshape(half_rows, BLK)
    f_half = potential(merged(partial) - PER2 * squares)
    col_bias = (
        OFFSET * f_half
        + (EPSILON * OFFSET) * w_half.reshape(half_rows, BLK)
        - squares
    )
    bias_rows = lax.all_gather(col_bias, plane, tiled=True)
    f_new = lax.all_gather(f_half, "core", tiled=True)

    col = local_call(
        column_kernel,
        4 * HALF,
        [pltpu.VMEM((136, BLK), jnp.float32), pltpu.VMEM((136, BLK), jnp.float32)],
        "columns",
    )(items, count, x_all, y_all, bias_rows)
    col = lax.all_to_all(
        col.reshape(4, HALF, BLK), "x", split_axis=0, concat_axis=0, tiled=True
    )
    g_half = potential(merged(col) - PER2 * y_squares.reshape(HALF, BLK))
    g_new = lax.all_gather(g_half, "core", tiled=True)
    return f_new.reshape(RB_DEV * BLK), g_new.reshape(TB_DEV * BLK)


def solution(mesh):
    fine = Mesh(mesh.devices.reshape(4, 8, 4, 2), ("x", "z", "y", "core"))
    src = ("x", "z", "y")
    placed = (
        P(None, src),
        P(src),
        P(None, src),
        P(src),
        P("core", src, None),
        P("core", src, None),
        P("core", src),
    )
    return jax.shard_map(
        on_device, mesh=fine, in_specs=placed, out_specs=(P(src), P(src)), check_vma=False
    )
```

time: 637 us -> 345 us (0.54)
  the two profiles are of different devices: /device:TPU:1 before, /device:TPU:41 now
where the time goes in v1:
time: 345 us
  waiting for transfers between devices  117 us (34%)
  blocking collectives  100 us (29%)
  Pallas kernels  82 us (24%)
  between operations  14.2 us (4%)
  starting transfers between devices  13.7 us (4%)
  other arithmetic  11.4 us (3%)
  local copies, waits for them, and re-layouts  5.88 us (2%)
    all_gather x1, waiting for transfers between devices, on_device(): x_all = lax.all_gather(x_half, plane)  97.3 us
    all_gather x1, blocking collectives, on_device(): bias_rows = lax.all_gather(col_bias, plane, tiled=True)  48.3 us
    pallas_call x1, Pallas kernels, on_device(): local_call(row_kernel, rows, [pltpu.VMEM((5, rows, BLK), jnp.float32)], '...  41.3 us
    pallas_call x1, Pallas kernels, on_device(): local_call(column_kernel, 4 * HALF, [pltpu.VMEM((136, BLK), jnp.float32),...  40.6 us
    all_gather x1, blocking collectives, on_device(): listed = lax.all_gather(listed.T, ('z', 'y'), axis=1, tiled=True)  37.1 us
    all_to_all x1, waiting for transfers between devices, on_device(): lax.all_to_all(partial.reshape(2 * lines, half_rows, BLK), plane, split_a...  16.9 us
    all_gather x1, blocking collectives, on_device(): bias_all = lax.all_gather(y_bias.reshape(HALF, BLK), 'x', tiled=True)  11.3 us
    all_to_all x1, starting transfers between devices, on_device(): lax.all_to_all(col.reshape(4, HALF, BLK), 'x', split_axis=0, concat_axis=...  7.46 us
  transfers between devices with their start and end apart: 4, of which 3 were waited for; matrix products, arithmetic and copies ran while one was open for 3% of the time, Pallas kernels for 0%

profile of v1, /device:TPU:41, one launch (start us, length us, event | category | flops | bytes accessed | tf_op | source)
XLA Modules:
  0.0 344.6 jit_solution(17638216089924176284)
XLA Ops:
  7.2 0.0 copy-start.2
  7.2 0.0 all-gather.8.cloned.1.call-start
  7.2 2.4 multiply_reduce_fusion
  9.6 0.0 all-gather.8.cloned.1.call-update
  9.7 0.0 all-gather.6.cloned.1.call-start
  9.7 1.7 multiply_reduce_fusion.1
  11.4 0.0 all-gather.6.cloned.1.call-update
  11.4 0.7 fusion.19
  12.2 37.1 %all-gather.2 = s32[32,16,8]{1,2,0:T(8,128)S(1)} all-gather(s32[1,16,8]{1,2,0:T(8,128)S(1)} %fusion.19), channel_id=1, replica_groups=mesh['x'=4,'z'=8,'y'=4,'core'=2] {'z','y'}, dimensions={0}, use_global_device_ids=true | all-gather | bytes 16896 | tf_op jit(solution)/shard_map/all_gather | solution.py:164
  49.3 0.1 reshape.56
  49.4 0.7 convert_reduce_fusion.1
  50.3 11.3 %all_gather.32.bias_ref = f32[128,256]{1,0:T(8,128)S(1)} all-gather(f32[32,256]{1,0:T(8,128)S(1)} %reshape.48), channel_id=1, replica_groups=mesh['x'=4,'z'=8,'y'=4,'core'=2] {'x'}, dimensions={0}, use_global_device_ids=true | all-gather | bytes 163840 | tf_op jit(solution)/shard_map/all_gather | solution.py:167
  61.5 0.1 select_reduce_fusion.1
  61.7 4.6 %select_reduce_fusion = s32[256]{0:T(256)S(1)} fusion(s32[8,512]{1,0:T(8,128)S(1)} %get-tuple-element.13, s32[8,512]{1,0:T(8,128)S(1)} %add_select_fusion.4), kind=kLoop, calls=%fused_computation | loop fusion | flops 3145472 | bytes 33792 | tf_op jit(solution)/shard_map/reduce_sum | solution.py:186
  66.3 0.6 compare_select_fusion.items_ref
  67.0 0.0 all-gather.8.cloned.1.call-done
  67.0 97.3 %all-gather.6.cloned.1.call-done = bf16[4096,2048]{1,0:T(8,128)(2,1)} async-done(((bf16[64,2048]{1,0:T(8,128)(2,1)}), bf16[4096,2048]{1,0:T(8,128)(2,1)}) %all-gather.6.cloned.1.call-update) | async-done | bytes 16777232 | tf_op jit(solution)/shard_map/all_gather | solution.py:165
  164.3 2.2 copy-done
  166.5 41.3 %rows.1 = f32[512,256]{1,0:T(8,128)} custom-call(s32[256]{0:T(256)S(1)} %compare_select_fusion.items_ref, s32[1]{0:T(128)} %bitcast.10.count_ref, bf16[64,64,2048]{2,1,0:T(8,128)(2,1)} %bitcast.60, bf16[4,64,8192]{2,1,0:T(8,128)(2,1)S(1)} %bitcast.58, f32[128,256]{1,0:T(8,128)S(1)} %all_gather.32.bias_ref), custom_call_target="tpu_custom_call" | custom-call | tf_op jit(solution)/shard_map/rows/pallas_call | solution.py:193
  207.8 6.2 %all-to-all-start = ((f32[64,8,256]{2,1,0:T(8,128)}), f32[64,8,256]{2,1,0:T(8,128)S(1)}, u32[]{:S(2)}, u32[]{:S(2)}) async-start(f32[64,8,256]{2,1,0:T(8,128)} %bitcast.13), calls=%async_computation | async-start | bytes 1048576 | tf_op jit(solution)/shard_map/all_to_all | solution.py:196
  214.1 16.9 %all-to-all-done = f32[64,8,256]{2,1,0:T(8,128)S(1)} async-done(((f32[64,8,256]{2,1,0:T(8,128)}), f32[64,8,256]{2,1,0:T(8,128)S(1)}, u32[]{:S(2)}, u32[]{:S(2)}) %all-to-all-start) | async-done | bytes 524320 | tf_op jit(solution)/shard_map/all_to_all | solution.py:196
  231.0 0.1 reduce_max.18
  231.1 0.1 exponential_reduce_fusion
  231.3 48.3 %all_gather.34.bias_ref = f32[512,256]{1,0:T(8,128)S(1)} all-gather(f32[8,256]{1,0:T(8,128)S(1)} %get-tuple-element.11), channel_id=1, replica_groups=mesh['x'=4,'z'=8,'y'=4,'core'=2] {'z','y','core'}, dimensions={0}, use_global_device_ids=true | all-gather | bytes 532480 | tf_op jit(solution)/shard_map/all_gather | solution.py:206
  279.5 2.2 copy-done.1
  281.7 40.6 %columns.1 = f32[128,256]{1,0:T(8,128)} custom-call(s32[256]{0:T(256)S(1)} %compare_select_fusion.items_ref, s32[1]{0:T(128)} %bitcast.10.count_ref, bf16[64,64,2048]{2,1,0:T(8,128)(2,1)} %bitcast.61, bf16[4,64,8192]{2,1,0:T(8,128)(2,1)S(1)} %bitcast.59, f32[512,256]{1,0:T(8,128)S(1)} %all_gather.34.bias_ref), custom_call_target="tpu_custom_call" | custom-call | tf_op jit(solution)/shard_map/columns/pallas_call | solution.py:209
  322.4 7.5 %all-to-all-start.1 = ((f32[4,32,256]{2,1,0:T(8,128)}), f32[4,32,256]{2,1,0:T(8,128)S(1)}, u32[]{:S(2)}, u32[]{:S(2)}) async-start(f32[4,32,256]{2,1,0:T(8,128)} %bitcast.14), calls=%async_computation.1 | async-start | bytes 262144 | tf_op jit(solution)/shard_map/all_to_all | solution.py:215
  329.8 1.8 all_gather.33
  331.7 0.6 copy.14
  332.3 2.8 all-to-all-done.1
  335.2 1.9 all_gather.35
  337.1 0.7 copy.15
  (30 shorter events, 0.4 us)
Async XLA Ops:
  7.2 42.9 %copy-start.2 = (bf16[16384]{0:T(1024)(128)(2,1)S(1)}, bf16[16384]{0:T(1024)(128)(2,1)}, u32[]{:S(2)}) copy-start(bf16[16384]{0:T(1024)(128)(2,1)} %param.10) | copy-start | bytes 98308
  7.2 59.8 %all-gather.8.cloned.1.call-start = ((), (), s32[]{:S(2)}) async-start(), calls=%async_computation.3 | async-start | bytes 5242880 | tf_op jit(solution)/shard_map/all_gather | solution.py:166
  9.7 154.6 %all-gather.6.cloned.1.call-start = ((), (), s32[]{:S(2)}) async-start(), calls=%async_computation.2 | async-start | bytes 17039360 | tf_op jit(solution)/shard_map/all_gather | solution.py:165
  164.3 2.2 copy-start
  166.5 47.6 %copy-start.3 = (f32[4096]{0:T(1024)S(1)}, f32[4096]{0:T(1024)}, u32[]{:S(2)}) copy-start(f32[4096]{0:T(1024)} %param.8) | copy-start | bytes 49156
  207.8 23.2 %all-to-all-start = ((f32[64,8,256]{2,1,0:T(8,128)}), f32[64,8,256]{2,1,0:T(8,128)S(1)}, u32[]{:S(2)}, u32[]{:S(2)}) async-start(f32[64,8,256]{2,1,0:T(8,128)} %bitcast.13), calls=%async_computation | async-start | bytes 1048576 | tf_op jit(solution)/shard_map/all_to_all | solution.py:196
  279.5 2.2 copy-start.1
  322.4 12.7 %all-to-all-start.1 = ((f32[4,32,256]{2,1,0:T(8,128)}), f32[4,32,256]{2,1,0:T(8,128)S(1)}, u32[]{:S(2)}, u32[]{:S(2)}) async-start(f32[4,32,256]{2,1,0:T(8,128)} %bitcast.14), calls=%async_computation.1 | async-start | bytes 262144 | tf_op jit(solution)/shard_map/all_to_all | solution.py:215
Sparse Core Ops, SparseCore 0:
  9.8 53.9 all-gather.7
  66.6 97.6 all-gather.5

commit v2 on v1

v2 whole, which is shorter than its diff:
```python
import functools
import heapq

import jax
import jax.numpy as jnp
import numpy as np
from jax import lax
from jax.experimental import pallas as pl
from jax.experimental.pallas import tpu as pltpu
from jax.sharding import Mesh, PartitionSpec as P

DIM = 64
BLK = 256
KH = 8
RB_DEV = 16
TB_DEV = 64
HALF = TB_DEV // 2

EPSILON = 0.1
EMPTY = -1e30
PER = 2.0 / (DIM * EPSILON)
PER2 = PER * float(np.log2(np.e))
OFFSET = DIM / 2.0
LN2 = float(np.log(2.0))
AUG = 16
UNROLL = 2


def split3(row):
    high = row.astype(jnp.bfloat16).astype(jnp.float32)
    middle = (row - high).astype(jnp.bfloat16).astype(jnp.float32)
    low = row - high - middle
    at = lax.broadcasted_iota(jnp.int32, (AUG, BLK), 0)
    rows = jnp.where(at == 0, high, jnp.where(at == 1, middle, jnp.where(at == 2, low, 0.0)))
    return rows.astype(jnp.bfloat16)


def three_ones():
    at = lax.broadcasted_iota(jnp.int32, (AUG, BLK), 0)
    return jnp.where(at < 3, 1.0, 0.0).astype(jnp.bfloat16)


def tile_logits(left, right):
    return lax.dot_general(
        left, right, (((0,), (0,)), ((), ())), preferred_element_type=jnp.float32
    )


def peak_and_mass(tile):
    peak = jnp.max(tile, axis=0, keepdims=True)
    mass = jnp.sum(jnp.exp2((tile - peak) * PER2), axis=0, keepdims=True)
    return peak, mass


def lane_block(index):
    return pl.ds(pl.multiple_of(index * BLK, BLK), BLK)


def x_tile(x_ref, block):
    return x_ref[block // KH, :, lane_block(block % KH)]


def y_tile(y_ref, block):
    return y_ref[block // HALF, :, lane_block(block % HALF)]


def row_kernel(items_ref, x_ref, y_ref, bias_ref, out_ref, slots):
    slots[...] = jnp.full(slots.shape, EMPTY, jnp.float32)
    ones = three_ones()

    def step(group, carry):
        for k in range(UNROLL):
            code = items_ref[0, group * UNROLL + k]
            row, col = code // 256, code % 256
            safe = col % 128
            left = jnp.concatenate(
                [y_tile(y_ref, safe), split3(bias_ref[pl.ds(safe, 1), :])], axis=0
            )
            right = jnp.concatenate([x_tile(x_ref, row), ones], axis=0)
            peak, mass = peak_and_mass(tile_logits(left, right))
            slots[col // HALF, pl.ds(row, 1), :] = peak * PER2 + jnp.log2(mass)
        return carry

    lax.fori_loop(0, (items_ref[1, 0] + UNROLL - 1) // UNROLL, step, 0)
    parts = [slots[k] for k in range(4)]
    top = jnp.maximum(jnp.maximum(parts[0], parts[1]), jnp.maximum(parts[2], parts[3]))
    total = sum(jnp.exp2(part - top) for part in parts)
    out_ref[...] = top + jnp.log2(total)


def column_kernel(items_ref, x_ref, y_ref, bias_ref, out_ref, peaks, masses):
    peaks[...] = jnp.full(peaks.shape, EMPTY, jnp.float32)
    masses[...] = jnp.zeros(masses.shape, jnp.float32)
    ones = three_ones()

    def step(group, carry):
        for k in range(UNROLL):
            code = items_ref[0, group * UNROLL + k]
            row, col = code // 256, code % 256
            left = jnp.concatenate(
                [x_tile(x_ref, row), split3(bias_ref[pl.ds(row, 1), :])], axis=0
            )
            right = jnp.concatenate([y_tile(y_ref, col % 128), ones], axis=0)
            peak, mass = peak_and_mass(tile_logits(left, right))
            old = peaks[pl.ds(col, 1), :]
            new = jnp.maximum(old, peak)
            peaks[pl.ds(col, 1), :] = new
            masses[pl.ds(col, 1), :] = masses[pl.ds(col, 1), :] * jnp.exp2(
                (old - new) * PER2
            ) + mass * jnp.exp2((peak - new) * PER2)
        return carry

    lax.fori_loop(0, (items_ref[1, 0] + UNROLL - 1) // UNROLL, step, 0)
    mass = masses[0:128, :]
    out_ref[...] = jnp.where(mass > 0.0, peaks[0:128, :] * PER2 + jnp.log2(mass), EMPTY)


SMEM = pl.BlockSpec(memory_space=pltpu.SMEM)
VMEM = pl.BlockSpec(memory_space=pltpu.VMEM)


def local_call(body, out_rows, scratch, name):
    return pl.pallas_call(
        body,
        out_shape=jax.ShapeDtypeStruct((out_rows, BLK), jnp.float32),
        in_specs=[SMEM, VMEM, VMEM, VMEM],
        out_specs=VMEM,
        scratch_shapes=scratch,
        compiler_params=pltpu.CompilerParams(vmem_limit_bytes=48 * 1024 * 1024),
        name=name,
    )


MESH = pl.DeviceIdType.MESH
NX, NZ, NY, NC = 4, 8, 4, 2
LINES = NZ * NY
ROWS = LINES * RB_DEV
HALF_RB = RB_DEV // 2
MOST = LINES * KH
X_LANES = HALF_RB * BLK
Y_LANES = HALF * BLK
A_LANES = 3 * BLK
B_LANES = X_LANES - A_LANES
Y_CHUNKS = 4
CHUNK = Y_LANES // Y_CHUNKS


def anywhere():
    return pl.BlockSpec(memory_space=pl.ANY)


def place():
    return tuple(lax.axis_index(axis) for axis in ("x", "z", "y", "core"))


def moved(size, offset):
    longest = {8: 4, 4: 2}[size]
    shortest = size - 1 - longest
    out = []
    if -longest < offset <= 0:
        out.append((1, offset - 1))
    if 0 <= offset < shortest:
        out.append((-1, offset + 1))
    return out


def onward(piece):
    kind, a, b = piece
    if kind == "A":
        found = [("z", d, ("A", n, b)) for d, n in moved(NZ, a)]
        if a == 0:
            found += [("y", d, ("A", 0, n)) for d, n in moved(NY, b)]
    elif kind == "B":
        found = [("z", d, ("B", n, 0)) for d, n in moved(NZ, a)] if b == 0 else []
        found += [("y", d, ("B", a, n)) for d, n in moved(NY, b)]
    else:
        found = [("x", d, (kind, n, 0)) for d, n in moved(NX, a)]
    return found


def gather_plan():
    took = {"A": 2.0, "B": 2.0 * B_LANES / A_LANES, "Y": 2.0 * CHUNK / A_LANES}
    kinds = [f"Y{k}" for k in range(Y_CHUNKS)]
    first = [("B", 0, 0), ("A", 0, 0)] + [(k, 0, 0) for k in kinds]
    free, waiting, order = {}, [], []

    def send(now, piece):
        for axis, direction, seen in onward(piece):
            begin = max(now, free.get((axis, direction), 0.0))
            end = begin + took[piece[0][0]]
            free[axis, direction] = end
            heapq.heappush(waiting, (end + 1.0, seen))

    for piece in first:
        send(0.0, piece)
    while waiting:
        now, piece = heapq.heappop(waiting)
        order.append(piece)
        send(now, piece)
    return first, order


def gather_kernel(
    x_ref, y_ref, g_ref, list_ref,
    x_all, y_all, bias_all, squares_ref, items_ref,
    codes, x_own, y_own, bias_sem, code_sem, own_sem, keep_sem, x_send, y_send, pair_send, pair_recv, got,
):
    x, z, y, c = place()
    turn = 1 - 2 * c
    line = z * NY + y
    first, order = gather_plan()
    index = {piece: k for k, piece in enumerate(order)}

    barrier = pltpu.get_barrier_semaphore()

    def plane_peer(k):
        other = lax.rem(line + k, LINES)
        return (x, other // NY, other % NY, c)

    def greet(k, carry):
        pl.semaphore_signal(barrier, inc=1, device_id=plane_peer(k), device_id_type=MESH)
        return carry

    lax.fori_loop(1, LINES, greet, 0)
    for k in range(1, NX):
        pl.semaphore_signal(
            barrier, inc=1, device_id=(lax.rem(x + k, NX), z, y, c), device_id_type=MESH
        )
    sibling = (x, z, y, 1 - c)
    pl.semaphore_signal(barrier, inc=1, device_id=sibling, device_id_type=MESH)

    x_mine = pl.multiple_of(c * X_LANES, X_LANES)
    y_mine = pl.multiple_of(c * Y_LANES, Y_LANES)
    keeps = [
        pltpu.make_async_copy(
            x_ref.at[:, pl.ds(k * X_LANES, X_LANES)], x_all.at[line * 2 + k], keep_sem.at[k]
        )
        for k in range(2)
    ]
    keeps.append(
        pltpu.make_async_copy(y_ref.at[:, pl.ds(y_mine, Y_LANES)], y_all.at[x], keep_sem.at[2])
    )
    owns = [
        pltpu.make_async_copy(x_ref.at[:, pl.ds(x_mine, X_LANES)], x_own, own_sem.at[0]),
        pltpu.make_async_copy(y_ref.at[:, pl.ds(y_mine, Y_LANES)], y_own, own_sem.at[1]),
    ]
    for copy in owns + keeps:
        copy.start()
    pl.semaphore_wait(barrier, LINES - 1 + NX - 1 + 1)

    def lanes_of(kind):
        if kind == "A":
            return 0, A_LANES
        if kind == "B":
            return A_LANES, B_LANES
        return int(kind[1:]) * CHUNK, CHUNK

    def slot(piece):
        kind, a, b = piece
        begin, width = lanes_of(kind)
        if kind[0] == "Y":
            return y_all.at[lax.rem(x + turn * a + NX, NX), :, pl.ds(begin, width)]
        origin = lax.rem(z + turn * a + NZ, NZ) * NY + lax.rem(y + turn * b + NY, NY)
        return x_all.at[origin * 2 + c, :, pl.ds(begin, width)]

    def source(piece):
        kind, a, b = piece
        if a or b:
            return slot(piece)
        begin, width = lanes_of(kind)
        if kind[0] == "Y":
            return y_ref.at[:, pl.ds(pl.multiple_of(y_mine + begin, BLK), width)]
        return x_ref.at[:, pl.ds(pl.multiple_of(x_mine + begin, BLK), width)]

    def neighbour(axis, direction):
        step = turn * direction
        return (
            lax.rem(x + step + NX, NX) if axis == "x" else x,
            lax.rem(z + step + NZ, NZ) if axis == "z" else z,
            lax.rem(y + step + NY, NY) if axis == "y" else y,
            c,
        )

    def pass_on(piece):
        for axis, direction, seen in onward(piece):
            pltpu.make_async_remote_copy(
                src_ref=source(piece),
                dst_ref=slot(piece),
                send_sem=y_send if piece[0][0] == "Y" else x_send,
                recv_sem=got.at[index[seen]],
                device_id=neighbour(axis, direction),
                device_id_type=MESH,
            ).start()

    for piece in first:
        pass_on(piece)

    def send_codes(k, carry):
        pltpu.make_async_remote_copy(
            src_ref=list_ref,
            dst_ref=codes.at[line],
            send_sem=code_sem.at[0],
            recv_sem=code_sem.at[1],
            device_id=plane_peer(k),
            device_id_type=MESH,
        ).start()
        return carry

    lax.fori_loop(1, LINES, send_codes, 0)

    for copy in owns:
        copy.wait()

    def squares_of(tile):
        return 0.5 * jnp.sum(jnp.square(tile.astype(jnp.float32)), axis=0, keepdims=True)

    for k in range(HALF_RB):
        squares_ref[k : k + 1, :] = squares_of(x_own[:, k * BLK : (k + 1) * BLK])
    y_squares = [squares_of(y_own[:, k * BLK : (k + 1) * BLK]) for k in range(HALF)]
    for k in range(HALF):
        squares_ref[HALF_RB + k : HALF_RB + k + 1, :] = y_squares[k]
    own_bias = OFFSET * g_ref[...].astype(jnp.float32) - squares_ref[HALF_RB : HALF_RB + HALF, :]
    bias_all[x] = own_bias
    for k in range(1, NX):
        pltpu.make_async_remote_copy(
            src_ref=bias_all.at[x],
            dst_ref=bias_all.at[x],
            send_sem=bias_sem.at[0],
            recv_sem=bias_sem.at[1],
            device_id=(lax.rem(x + k, NX), z, y, c),
            device_id_type=MESH,
        ).start()

    def advance(pieces):
        for piece in pieces:
            here = slot(piece)
            pltpu.make_async_copy(here, here, got.at[index[piece]]).wait()
            pass_on(piece)
            if piece[0][0] != "Y":
                pltpu.make_async_remote_copy(
                    src_ref=here,
                    dst_ref=here,
                    send_sem=pair_send,
                    recv_sem=pair_recv,
                    device_id=sibling,
                    device_id_type=MESH,
                ).start()

    third = len(order) // 3
    advance(order[:third])

    codes[line] = list_ref[...]
    for side in range(2):
        pltpu.make_async_copy(
            codes.at[pl.ds(0, LINES - 1)], codes.at[pl.ds(0, LINES - 1)], code_sem.at[side]
        ).wait()
    table = codes[...].reshape(LINES, RB_DEV * KH)
    owner = table // HALF
    match = (table >= 0) & (owner % LINES == line)
    lane = lax.broadcasted_iota(jnp.int32, table.shape, 1)
    row = lax.broadcasted_iota(jnp.int32, table.shape, 0) * RB_DEV + lane // KH
    code = (row * 256 + (owner // LINES) * HALF + table % HALF).astype(jnp.float32)
    hits = match.astype(jnp.float32)
    wide = RB_DEV * KH
    over, down = (lax.broadcasted_iota(jnp.int32, (wide, wide), k) for k in range(2))
    exact = functools.partial(
        jnp.dot, preferred_element_type=jnp.float32, precision=lax.Precision.HIGHEST
    )
    left = exact(hits, (over < down).astype(jnp.float32))
    totals = exact(hits, jnp.ones((wide, wide), jnp.float32))
    over, down = (lax.broadcasted_iota(jnp.int32, (LINES, LINES), k) for k in range(2))
    above = exact((down < over).astype(jnp.float32), totals)
    count = jnp.sum(totals, axis=0, keepdims=True)
    spot_of = jnp.where(match, left + above, -1.0)
    spots = lax.broadcasted_iota(jnp.int32, (MOST, wide), 0).astype(jnp.float32)
    found = jnp.zeros((MOST, wide), jnp.float32)
    for k in range(LINES):
        found += jnp.where(spot_of[k : k + 1, :] == spots, code[k : k + 1, :], 0.0)
    items = lax.dot_general(
        jnp.ones((8, wide), jnp.float32),
        found,
        (((1,), (1,)), ((), ())),
        preferred_element_type=jnp.float32,
        precision=lax.Precision.HIGHEST,
    )
    many = jnp.concatenate([count] * (MOST // wide), axis=1)
    spot = lax.broadcasted_iota(jnp.int32, (8, MOST), 1).astype(jnp.float32)
    items = jnp.where(spot < many, items, 128.0)
    at = lax.broadcasted_iota(jnp.int32, (8, MOST), 0)
    items_ref[...] = jnp.where(at == 0, items, many).astype(jnp.int32)

    advance(order[third:])
    for copy in keeps:
        copy.wait()
    most_x = x_all.at[pl.ds(0, LINES - 1)]
    for semaphore in (x_send, pair_send, pair_recv):
        pltpu.make_async_copy(most_x, most_x, semaphore).wait()
    most_y = y_all.at[pl.ds(0, NX - 1)]
    pltpu.make_async_copy(most_y, most_y, y_send).wait()
    most_bias = bias_all.at[pl.ds(0, NX - 1)]
    for side in range(2):
        pltpu.make_async_copy(most_bias, most_bias, bias_sem.at[side]).wait()


def gather(x_src, y_tgt, g_half, listed):
    count = len(gather_plan()[1])
    dma = pltpu.SemaphoreType.DMA
    return pl.pallas_call(
        gather_kernel,
        out_shape=(
            jax.ShapeDtypeStruct((2 * LINES, DIM, X_LANES), jnp.bfloat16),
            jax.ShapeDtypeStruct((NX, DIM, Y_LANES), jnp.bfloat16),
            jax.ShapeDtypeStruct((NX, HALF, BLK), jnp.float32),
            jax.ShapeDtypeStruct((HALF_RB + HALF, BLK), jnp.float32),
            jax.ShapeDtypeStruct((8, MOST), jnp.int32),
        ),
        in_specs=[anywhere(), anywhere(), VMEM, VMEM],
        out_specs=(anywhere(), anywhere(), VMEM, VMEM, VMEM),
        scratch_shapes=[
            pltpu.VMEM((LINES, 1, RB_DEV * KH), jnp.int32),
            pltpu.VMEM((DIM, X_LANES), jnp.bfloat16),
            pltpu.VMEM((DIM, Y_LANES), jnp.bfloat16),
            dma((2,)),
            dma((2,)),
            dma((2,)),
            dma((3,)),
            dma,
            dma,
            dma,
            dma,
            dma((count,)),
        ],
        compiler_params=pltpu.CompilerParams(
            collective_id=0, has_side_effects=True, vmem_limit_bytes=24 * 1024 * 1024
        ),
        name="gather",
    )(x_src, y_tgt, g_half, listed)


def potential(logit2):
    logit = logit2 * LN2
    top = jnp.maximum(logit, 0.0)
    return -EPSILON * (top + jnp.log(jnp.exp(-top) + jnp.exp(logit - top)))


def merged(parts):
    top = functools.reduce(jnp.maximum, parts)
    return top + jnp.log2(sum(jnp.exp2(part - top) for part in parts))


def exchange_kernel(
    part_ref, w_ref, squares_ref, f_ref, bias_ref, parts, part_sem, bias_sem, f_sem
):
    x, z, y, c = place()
    group = NC * LINES
    me = (z * NY + y) * NC + c

    def peer(k):
        other = lax.rem(me + k, group)
        return other, (x, other // (NY * NC), (other // NC) % NY, other % NC)

    barrier = pltpu.get_barrier_semaphore()

    def greet(k, carry):
        pl.semaphore_signal(barrier, inc=1, device_id=peer(k)[1], device_id_type=MESH)
        return carry

    lax.fori_loop(1, group, greet, 0)
    pl.semaphore_wait(barrier, group - 1)

    def send_part(k, carry):
        other, device = peer(k)
        pltpu.make_async_remote_copy(
            src_ref=part_ref.at[other],
            dst_ref=parts.at[me],
            send_sem=part_sem.at[0],
            recv_sem=part_sem.at[1],
            device_id=device,
            device_id_type=MESH,
        ).start()
        return carry

    lax.fori_loop(1, group, send_part, 0)
    parts[me] = part_ref[me]
    others = parts.at[pl.ds(0, group - 1)]
    pltpu.make_async_copy(others, others, part_sem.at[1]).wait()
    squares = squares_ref[...]
    f_half = potential(merged([parts[k] for k in range(group)]) - PER2 * squares)
    mine = pl.ds(pl.multiple_of(c * HALF_RB, HALF_RB), HALF_RB)
    f_ref[mine, :] = f_half
    bias_ref[me] = OFFSET * f_half + (EPSILON * OFFSET) * w_ref[mine, :] - squares

    def send_bias(k, carry):
        pltpu.make_async_remote_copy(
            src_ref=bias_ref.at[me],
            dst_ref=bias_ref.at[me],
            send_sem=bias_sem.at[0],
            recv_sem=bias_sem.at[1],
            device_id=peer(k)[1],
            device_id_type=MESH,
        ).start()
        return carry

    lax.fori_loop(1, group, send_bias, 0)
    over = pltpu.make_async_remote_copy(
        src_ref=f_ref.at[mine, :],
        dst_ref=f_ref.at[mine, :],
        send_sem=f_sem.at[0],
        recv_sem=f_sem.at[1],
        device_id=(x, z, y, 1 - c),
        device_id_type=MESH,
    )
    over.start()
    pltpu.make_async_copy(others, others, part_sem.at[0]).wait()
    others = bias_ref.at[pl.ds(0, group - 1)]
    for side in range(2):
        pltpu.make_async_copy(others, others, bias_sem.at[side]).wait()
    over.wait()


def exchange(partial, w_rows, squares):
    dma = pltpu.SemaphoreType.DMA
    group = NC * LINES
    return pl.pallas_call(
        exchange_kernel,
        out_shape=(
            jax.ShapeDtypeStruct((RB_DEV, BLK), jnp.float32),
            jax.ShapeDtypeStruct((group, HALF_RB, BLK), jnp.float32),
        ),
        in_specs=[VMEM, VMEM, VMEM],
        out_specs=(VMEM, VMEM),
        scratch_shapes=[
            pltpu.VMEM((group, HALF_RB, BLK), jnp.float32),
            dma((2,)),
            dma((2,)),
            dma((2,)),
        ],
        compiler_params=pltpu.CompilerParams(
            collective_id=1, has_side_effects=True, vmem_limit_bytes=16 * 1024 * 1024
        ),
        name="exchange",
    )(partial, w_rows, squares)


def finish_kernel(part_ref, squares_ref, g_ref, parts, part_sem, g_sem):
    x, z, y, c = place()
    barrier = pltpu.get_barrier_semaphore()
    peers = [(lax.rem(x + k, NX), z, y, c) for k in range(1, NX)]
    sibling = (x, z, y, 1 - c)
    for device in peers + [sibling]:
        pl.semaphore_signal(barrier, inc=1, device_id=device, device_id_type=MESH)
    pl.semaphore_wait(barrier, NX)
    for device in peers:
        pltpu.make_async_remote_copy(
            src_ref=part_ref.at[device[0]],
            dst_ref=parts.at[x],
            send_sem=part_sem.at[0],
            recv_sem=part_sem.at[1],
            device_id=device,
            device_id_type=MESH,
        ).start()
    parts[x] = part_ref[x]
    others = parts.at[pl.ds(0, NX - 1)]
    pltpu.make_async_copy(others, others, part_sem.at[1]).wait()
    g_half = potential(merged([parts[k] for k in range(NX)]) - PER2 * squares_ref[...])
    mine = pl.ds(pl.multiple_of(c * HALF, HALF), HALF)
    g_ref[mine, :] = g_half
    over = pltpu.make_async_remote_copy(
        src_ref=g_ref.at[mine, :],
        dst_ref=g_ref.at[mine, :],
        send_sem=g_sem.at[0],
        recv_sem=g_sem.at[1],
        device_id=sibling,
        device_id_type=MESH,
    )
    over.start()
    pltpu.make_async_copy(others, others, part_sem.at[0]).wait()
    over.wait()


def finish(partial, squares):
    dma = pltpu.SemaphoreType.DMA
    return pl.pallas_call(
        finish_kernel,
        out_shape=jax.ShapeDtypeStruct((TB_DEV, BLK), jnp.float32),
        in_specs=[VMEM, VMEM],
        out_specs=VMEM,
        scratch_shapes=[pltpu.VMEM((NX, HALF, BLK), jnp.float32), dma((2,)), dma((2,))],
        compiler_params=pltpu.CompilerParams(collective_id=2, has_side_effects=True),
        name="finish",
    )(partial, squares)


def on_device(x_src, w_src, y_tgt, g_in, support_owner, support_local, live_count):
    core = lax.axis_index("core")
    live = lax.broadcasted_iota(jnp.int32, (RB_DEV, KH), 1) < live_count[0][:, None]
    listed = jnp.where(live, support_owner[0] * HALF + support_local[0], -1)
    g_half = lax.dynamic_slice_in_dim(g_in.reshape(TB_DEV, BLK), core * HALF, HALF, 0)
    x_all, y_all, bias_all, squares, items = gather(
        x_src, y_tgt, g_half, listed.reshape(1, RB_DEV * KH)
    )
    partial = local_call(
        row_kernel, ROWS, [pltpu.VMEM((5, ROWS, BLK), jnp.float32)], "rows"
    )(items, x_all, y_all, bias_all.reshape(NX * HALF, BLK))
    f_new, bias_rows = exchange(
        partial.reshape(NC * LINES, HALF_RB, BLK), w_src.reshape(RB_DEV, BLK), squares[:HALF_RB]
    )
    col = local_call(
        column_kernel,
        NX * HALF,
        [pltpu.VMEM((136, BLK), jnp.float32), pltpu.VMEM((136, BLK), jnp.float32)],
        "columns",
    )(items, x_all, y_all, bias_rows.reshape(ROWS, BLK))
    g_new = finish(col.reshape(NX, HALF, BLK), squares[HALF_RB:])
    return f_new.reshape(RB_DEV * BLK), g_new.reshape(TB_DEV * BLK)


def solution(mesh):
    fine = Mesh(mesh.devices.reshape(NX, NZ, NY, NC), ("x", "z", "y", "core"))
    src = ("x", "z", "y")
    placed = (
        P(None, src),
        P(src),
        P(None, src),
        P(src),
        P("core", src, None),
        P("core", src, None),
        P("core", src),
    )
    return jax.shard_map(
        on_device, mesh=fine, in_specs=placed, out_specs=(P(src), P(src)), check_vma=False
    )
```

time: 345 us -> 193 us (0.56)
  the two profiles are of different devices: /device:TPU:41 before, /device:TPU:9 now
where the time goes in v2:
time: 193 us; the launch traced here: 192 us
  Pallas kernels  177 us (92%)
  local copies, waits for them, and re-layouts  13.5 us (7%)
    pallas_call x1, Pallas kernels, gather(): pl.pallas_call(gather_kernel, out_shape=(jax.ShapeDtypeStruct((2 * LINES,...  67.1 us
    pallas_call x1, Pallas kernels, exchange(): pl.pallas_call(exchange_kernel, out_shape=(jax.ShapeDtypeStruct((RB_DEV,...  40.2 us
    pallas_call x1, Pallas kernels, on_device(): local_call(row_kernel, ROWS, [pltpu.VMEM((5, ROWS, BLK), jnp.float32)], '...  29.7 us
    pallas_call x1, Pallas kernels, on_device(): local_call(column_kernel, NX * HALF, [pltpu.VMEM((136, BLK), jnp.float32)...  28.9 us
    unnamed x10, local copies, waits for them, and re-layouts  11.1 us
    pallas_call x1, Pallas kernels, finish(): pl.pallas_call(finish_kernel, out_shape=jax.ShapeDtypeStruct((TB_DEV, BLK...  10.8 us

profile of v2, /device:TPU:9, one launch (start us, length us, event | category | flops | bytes accessed | tf_op | source)
XLA Modules:
  0.0 192.4 jit_solution(11004561917841920574)
XLA Ops:
  0.6 0.7 iota_compare_fusion
  1.4 0.1 lt.27
  1.5 0.7 multiply_add_fusion
  2.2 0.1 copy.10
  2.2 0.1 add.18
  2.3 0.7 reshape.81.w_ref
  3.1 0.8 reshape.78
  3.9 0.0 copy-start.1
  3.9 1.6 copy-done.1
  5.5 0.0 copy-start.3
  5.5 1.0 copy-done.3
  6.5 67.1 %gather.1 = (bf16[64,64,2048]{2,1,0:T(8,128)(2,1)S(1)}, bf16[4,64,8192]{2,1,0:T(8,128)(2,1)S(1)}, f32[4,32,256]{2,1,0:T(8,128)S(1)}, f32[40,256]{1,0:T(8,128)S(1)}, s32[8,256]{1,0:T(8,128)S(1)}) custom-call(bf16[64,4096]{1,0:T(8,128)(2,1)S(1)} %copy-done.3, bf16[64,16384]{1,0:T(8,128)(2,1)S(1)} %copy-done.1, ...), custom_call_target="tpu_custom_call" | custom-call | tf_op jit(solution)/shard_map/gather/pallas_call | solution.py:408
  73.6 0.0 copy-start
  73.6 5.7 %copy-done = bf16[64,64,2048]{2,1,0:T(8,128)(2,1)} copy-done((bf16[64,64,2048]{2,1,0:T(8,128)(2,1)}, bf16[64,64,2048]{2,1,0:T(8,128)(2,1)S(1)}, u32[]{:S(2)}) %copy-start) | copy-done | bytes 16777240
  79.3 0.6 slice.7.squares_ref
  79.9 29.7 %rows.1 = f32[512,256]{1,0:T(8,128)S(1)} custom-call(s32[8,256]{1,0:T(8,128)S(1)} %get-tuple-element.9.items_ref, bf16[64,64,2048]{2,1,0:T(8,128)(2,1)} %copy-done, bf16[4,64,8192]{2,1,0:T(8,128)(2,1)S(1)} %get-tuple-element.11.y_ref, f32[128,256]{1,0:T(8,128)S(1)} %bitcast.12), custom_call_target="tpu_custom_call" | custom-call | tf_op jit(solution)/shard_map/rows/pallas_call | solution.py:602
  109.6 40.2 %exchange.1 = (f32[16,256]{1,0:T(8,128)S(1)}, f32[64,8,256]{2,1,0:T(8,128)S(1)}) custom-call(f32[64,8,256]{2,1,0:T(8,128)S(1)} %bitcast.9, f32[16,256]{1,0:T(8,128)S(1)} %reshape.81.w_ref, f32[8,256]{1,0:T(8,128)S(1)} %slice.6.squares_ref), custom_call_target="tpu_custom_call" | custom-call | tf_op jit(solution)/shard_map/exchange/pallas_call | solution.py:524
  149.9 0.6 copy.11
  150.5 28.9 %columns.1 = f32[128,256]{1,0:T(8,128)S(1)} custom-call(s32[8,256]{1,0:T(8,128)S(1)} %get-tuple-element.9.items_ref, bf16[64,64,2048]{2,1,0:T(8,128)(2,1)} %copy-done, bf16[4,64,8192]{2,1,0:T(8,128)(2,1)S(1)} %get-tuple-element.11.y_ref, f32[512,256]{1,0:T(8,128)S(1)} %bitcast.11), custom_call_target="tpu_custom_call" | custom-call | tf_op jit(solution)/shard_map/columns/pallas_call | solution.py:608
  179.4 0.0 copy-start.2
  179.4 0.6 copy-done.2
  180.1 10.8 %finish.1 = f32[64,256]{1,0:T(8,128)} custom-call(f32[4,32,256]{2,1,0:T(8,128)} %bitcast.10, f32[32,256]{1,0:T(8,128)} %slice.7.squares_ref), custom_call_target="tpu_custom_call" | custom-call | tf_op jit(solution)/shard_map/finish/pallas_call | solution.py:583
  190.9 1.5 copy.12
  (3 shorter events, 0.0 us)
Async XLA Ops:
  3.9 1.6 copy-start.1
  5.5 1.0 copy-start.3
  73.6 5.7 %copy-start = (bf16[64,64,2048]{2,1,0:T(8,128)(2,1)}, bf16[64,64,2048]{2,1,0:T(8,128)(2,1)S(1)}, u32[]{:S(2)}) copy-start(bf16[64,64,2048]{2,1,0:T(8,128)(2,1)S(1)} %get-tuple-element.10.x_ref) | copy-start | bytes 50331652
  179.4 0.6 copy-start.2

commit v3 on v2

v3 whole, which is shorter than its diff:
```python
import functools
import heapq

import jax
import jax.numpy as jnp
import numpy as np
from jax import lax
from jax.experimental import pallas as pl
from jax.experimental.pallas import tpu as pltpu
from jax.sharding import Mesh, PartitionSpec as P

DIM = 64
BLK = 256
KH = 8
RB_DEV = 16
TB_DEV = 64
HALF = TB_DEV // 2

EPSILON = 0.1
EMPTY = -1e30
PER = 2.0 / (DIM * EPSILON)
PER2 = PER * float(np.log2(np.e))
OFFSET = DIM / 2.0
LN2 = float(np.log(2.0))
AUG = 16

MESH = pl.DeviceIdType.MESH
NX, NZ, NY, NC = 4, 8, 4, 2
LINES = NZ * NY
HALF_RB = RB_DEV // 2
ROWS = LINES * HALF_RB
NONE = NX * TB_DEV
STRIDE = 2 * NONE
MOST = LINES * 2 * NX * NC
WIDE = RB_DEV * KH
X_LANES = HALF_RB * BLK
Y_LANES = HALF * BLK
UNROLL = 8


def split3(row):
    high = row.astype(jnp.bfloat16).astype(jnp.float32)
    middle = (row - high).astype(jnp.bfloat16).astype(jnp.float32)
    low = row - high - middle
    at = lax.broadcasted_iota(jnp.int32, (AUG, BLK), 0)
    rows = jnp.where(at == 0, high, jnp.where(at == 1, middle, jnp.where(at == 2, low, 0.0)))
    return rows.astype(jnp.bfloat16)


def three_ones():
    at = lax.broadcasted_iota(jnp.int32, (AUG, BLK), 0)
    return jnp.where(at < 3, 1.0, 0.0).astype(jnp.bfloat16)


def tile_logits(left, right):
    return lax.dot_general(
        left, right, (((0,), (0,)), ((), ())), preferred_element_type=jnp.float32
    )


def peak_and_mass(tile):
    peak = jnp.max(tile, axis=0, keepdims=True)
    mass = jnp.sum(jnp.exp2((tile - peak) * PER2), axis=0, keepdims=True)
    return peak, mass


def lane_block(index):
    return pl.ds(pl.multiple_of(index * BLK, BLK), BLK)


def x_tile(x_ref, block):
    return x_ref[block // HALF_RB, :, lane_block(block % HALF_RB)]


def y_tile(y_ref, block):
    return y_ref[block // TB_DEV, :, lane_block(block % TB_DEV)]


def for_pairs(items_ref, visit):
    def step(group, carry):
        for k in range(UNROLL):
            code = items_ref[0, group * UNROLL + k]
            visit(code // STRIDE, code % STRIDE)
        return carry

    lax.fori_loop(0, (items_ref[1, 0] + UNROLL - 1) // UNROLL, step, 0)


def row_kernel(items_ref, x_ref, y_ref, bias_ref, out_ref, slots):
    slots[...] = jnp.full(slots.shape, EMPTY, jnp.float32)
    ones = three_ones()

    def visit(row, col):
        safe = col % NONE
        left = jnp.concatenate(
            [y_tile(y_ref, safe), split3(bias_ref[pl.ds(safe, 1), :])], axis=0
        )
        right = jnp.concatenate([x_tile(x_ref, row), ones], axis=0)
        peak, mass = peak_and_mass(tile_logits(left, right))
        slots[col // HALF, pl.ds(row, 1), :] = peak * PER2 + jnp.log2(mass)

    for_pairs(items_ref, visit)
    out_ref[...] = merged([slots[k] for k in range(NC * NX)])


def column_kernel(items_ref, x_ref, y_ref, bias_ref, out_ref, peaks, masses):
    peaks[...] = jnp.full(peaks.shape, EMPTY, jnp.float32)
    masses[...] = jnp.zeros(masses.shape, jnp.float32)
    ones = three_ones()

    def visit(row, col):
        left = jnp.concatenate(
            [x_tile(x_ref, row), split3(bias_ref[pl.ds(row, 1), :])], axis=0
        )
        right = jnp.concatenate([y_tile(y_ref, col % NONE), ones], axis=0)
        peak, mass = peak_and_mass(tile_logits(left, right))
        old = peaks[pl.ds(col, 1), :]
        new = jnp.maximum(old, peak)
        peaks[pl.ds(col, 1), :] = new
        masses[pl.ds(col, 1), :] = masses[pl.ds(col, 1), :] * jnp.exp2(
            (old - new) * PER2
        ) + mass * jnp.exp2((peak - new) * PER2)

    for_pairs(items_ref, visit)
    mass = masses[0:NONE, :]
    out_ref[...] = jnp.where(mass > 0.0, peaks[0:NONE, :] * PER2 + jnp.log2(mass), EMPTY)


SMEM = pl.BlockSpec(memory_space=pltpu.SMEM)
VMEM = pl.BlockSpec(memory_space=pltpu.VMEM)


def local_call(body, out_rows, scratch, name):
    return pl.pallas_call(
        body,
        out_shape=jax.ShapeDtypeStruct((out_rows, BLK), jnp.float32),
        in_specs=[SMEM, VMEM, VMEM, VMEM],
        out_specs=VMEM,
        scratch_shapes=scratch,
        compiler_params=pltpu.CompilerParams(vmem_limit_bytes=26 * 1024 * 1024),
        name=name,
    )


A_LANES = 3 * BLK
B_LANES = X_LANES - A_LANES
Y_CHUNKS = 4
CHUNK = Y_LANES // Y_CHUNKS


def anywhere():
    return pl.BlockSpec(memory_space=pl.ANY)


def place():
    return tuple(lax.axis_index(axis) for axis in ("x", "z", "y", "core"))


def moved(size, offset):
    longest = {8: 4, 4: 2}[size]
    shortest = size - 1 - longest
    out = []
    if -longest < offset <= 0:
        out.append((1, offset - 1))
    if 0 <= offset < shortest:
        out.append((-1, offset + 1))
    return out


def onward(piece):
    kind, a, b = piece
    if kind == "A":
        found = [("z", d, ("A", n, b)) for d, n in moved(NZ, a)]
        if a == 0:
            found += [("y", d, ("A", 0, n)) for d, n in moved(NY, b)]
    elif kind == "B":
        found = [("z", d, ("B", n, 0)) for d, n in moved(NZ, a)] if b == 0 else []
        found += [("y", d, ("B", a, n)) for d, n in moved(NY, b)]
    else:
        found = [("x", d, (kind, n, 0)) for d, n in moved(NX, a)]
    return found


def gather_plan():
    took = {"A": 2.0, "B": 2.0 * B_LANES / A_LANES, "Y": 2.0 * CHUNK / A_LANES}
    kinds = [f"Y{k}" for k in range(Y_CHUNKS)]
    first = [("B", 0, 0), ("A", 0, 0)] + [(k, 0, 0) for k in kinds]
    free, waiting, order = {}, [], []

    def send(now, piece):
        for axis, direction, seen in onward(piece):
            begin = max(now, free.get((axis, direction), 0.0))
            end = begin + took[piece[0][0]]
            free[axis, direction] = end
            heapq.heappush(waiting, (end + 1.0, seen))

    for piece in first:
        send(0.0, piece)
    while waiting:
        now, piece = heapq.heappop(waiting)
        order.append(piece)
        send(now, piece)
    return first, order


def gather_kernel(
    x_ref, y_ref, g_ref, owner_ref, local_ref, live_ref,
    x_all, y_all, bias_all, squares_ref, items_ref,
    codes, x_own, y_own, bias_sem, code_sem, own_sem, keep_sem, x_send, y_send, pair_sem, got,
):
    x, z, y, c = place()
    turn = 1 - 2 * c
    line = z * NY + y
    group = LINES * NC
    me = line * NC + c
    first, order = gather_plan()
    index = {piece: k for k, piece in enumerate(order)}

    barrier = pltpu.get_barrier_semaphore()
    sibling = (x, z, y, 1 - c)

    def plane_peer(k):
        other = lax.rem(me + k, group)
        return (x, other // (NY * NC), (other // NC) % NY, other % NC)

    def greet(k, carry):
        pl.semaphore_signal(barrier, inc=1, device_id=plane_peer(k), device_id_type=MESH)
        return carry

    line_peers = [(lax.rem(x + k, NX), z, y, core) for k in range(1, NX) for core in range(NC)]
    for device in line_peers:
        pl.semaphore_signal(barrier, inc=1, device_id=device, device_id_type=MESH)
    lax.fori_loop(1, group, greet, 0)

    x_mine = pl.multiple_of(c * X_LANES, X_LANES)
    y_mine = pl.multiple_of(c * Y_LANES, Y_LANES)
    owns = [
        pltpu.make_async_copy(x_ref.at[:, pl.ds(x_mine, X_LANES)], x_own, own_sem.at[0]),
        pltpu.make_async_copy(y_ref.at[:, pl.ds(y_mine, Y_LANES)], y_own, own_sem.at[1]),
    ]
    keeps = [
        pltpu.make_async_copy(
            x_ref.at[:, pl.ds(x_mine, X_LANES)], x_all.at[line], keep_sem.at[0]
        ),
        pltpu.make_async_copy(y_ref, y_all.at[x], keep_sem.at[1]),
    ]
    for copy in owns + keeps:
        copy.start()

    exact = functools.partial(
        jnp.dot, preferred_element_type=jnp.float32, precision=lax.Precision.HIGHEST
    )
    down, over = (lax.broadcasted_iota(jnp.int32, (RB_DEV, KH), k) for k in range(2))
    live = jnp.zeros((RB_DEV, KH), jnp.int32)
    for r in range(RB_DEV):
        live = jnp.where(down == r, live_ref[0, r], live)
    listed = jnp.where(over < live, owner_ref[0] * HALF + local_ref[0], -1).astype(jnp.float32)
    down, over = (lax.broadcasted_iota(jnp.int32, (KH, WIDE), k) for k in range(2))
    spread = exact(listed, (over % KH == down).astype(jnp.float32))
    down, over = (lax.broadcasted_iota(jnp.int32, (RB_DEV, WIDE), k) for k in range(2))
    codes[me] = jnp.sum(
        jnp.where(over // KH == down, spread, 0.0), axis=0, keepdims=True
    ).astype(jnp.int32)
    pl.semaphore_wait(barrier, group - 1 + len(line_peers))

    def lanes_of(kind):
        if kind == "A":
            return 0, A_LANES
        if kind == "B":
            return A_LANES, B_LANES
        return int(kind[1:]) * CHUNK, CHUNK

    def slot(piece):
        kind, a, b = piece
        begin, width = lanes_of(kind)
        if kind[0] == "Y":
            there = pl.ds(pl.multiple_of(y_mine + begin, BLK), width)
            return y_all.at[lax.rem(x + turn * a + NX, NX), :, there]
        origin = lax.rem(z + turn * a + NZ, NZ) * NY + lax.rem(y + turn * b + NY, NY)
        return x_all.at[origin, :, pl.ds(begin, width)]

    def source(piece):
        kind, a, b = piece
        if a or b:
            return slot(piece)
        begin, width = lanes_of(kind)
        if kind[0] == "Y":
            return y_ref.at[:, pl.ds(pl.multiple_of(y_mine + begin, BLK), width)]
        return x_ref.at[:, pl.ds(pl.multiple_of(x_mine + begin, BLK), width)]

    def neighbour(axis, direction):
        step = turn * direction
        return (
            lax.rem(x + step + NX, NX) if axis == "x" else x,
            lax.rem(z + step + NZ, NZ) if axis == "z" else z,
            lax.rem(y + step + NY, NY) if axis == "y" else y,
            c,
        )

    def pass_on(piece):
        for axis, direction, seen in onward(piece):
            pltpu.make_async_remote_copy(
                src_ref=source(piece),
                dst_ref=slot(piece),
                send_sem=y_send if piece[0][0] == "Y" else x_send,
                recv_sem=got.at[index[seen]],
                device_id=neighbour(axis, direction),
                device_id_type=MESH,
            ).start()

    for piece in first:
        pass_on(piece)

    def send_codes(k, carry):
        pltpu.make_async_remote_copy(
            src_ref=codes.at[me],
            dst_ref=codes.at[me],
            send_sem=code_sem.at[0],
            recv_sem=code_sem.at[1],
            device_id=plane_peer(k),
            device_id_type=MESH,
        ).start()
        return carry

    lax.fori_loop(1, group, send_codes, 0)

    def squares_of(tile):
        return 0.5 * jnp.sum(jnp.square(tile.astype(jnp.float32)), axis=0, keepdims=True)

    def do_x_squares():
        owns[0].wait()
        for k in range(HALF_RB):
            squares_ref[k : k + 1, :] = squares_of(x_own[:, k * BLK : (k + 1) * BLK])
        owns[1].wait()

    def do_y_squares(begin):
        for k in range(begin, begin + 8):
            squares_ref[HALF_RB + k : HALF_RB + k + 1, :] = squares_of(
                y_own[:, k * BLK : (k + 1) * BLK]
            )

    def do_bias():
        g_half = jnp.where(c == 0, g_ref[:HALF, :], g_ref[HALF:, :])
        here = bias_all.at[x * NC + c]
        here[...] = OFFSET * g_half.astype(jnp.float32) - squares_ref[HALF_RB:, :]
        for device in line_peers + [sibling]:
            pltpu.make_async_remote_copy(
                src_ref=here,
                dst_ref=here,
                send_sem=bias_sem.at[0],
                recv_sem=bias_sem.at[1],
                device_id=device,
                device_id_type=MESH,
            ).start()

    table = {}
    steps = 4

    def do_table():
        for side in range(2):
            most = codes.at[pl.ds(0, group - 1)]
            pltpu.make_async_copy(most, most, code_sem.at[side]).wait()
        halves = [codes[pl.ds(k, LINES, stride=NC)].reshape(LINES, WIDE) for k in range(NC)]
        lane = lax.broadcasted_iota(jnp.int32, (LINES, WIDE), 1)
        turned = [pltpu.roll(part, WIDE // 2, 1) for part in halves]
        even = jnp.where(lane < WIDE // 2, halves[0], turned[1])
        odd = jnp.where(lane < WIDE // 2, turned[0], halves[1])
        entry = jnp.where(c == 0, even, odd)
        owner = entry // HALF
        match = (entry >= 0) & (owner % LINES == line)
        row = (
            lax.broadcasted_iota(jnp.int32, entry.shape, 0) * HALF_RB
            + lane % (WIDE // 2) // KH
        )
        col = owner // LINES * TB_DEV + lane // (WIDE // 2) * HALF + entry % HALF
        hits = match.astype(jnp.float32)
        down, over = (lax.broadcasted_iota(jnp.int32, (WIDE, WIDE), k) for k in range(2))
        left = exact(hits, (down < over).astype(jnp.float32))
        totals = exact(hits, jnp.ones((WIDE, WIDE), jnp.float32))
        down, over = (lax.broadcasted_iota(jnp.int32, (LINES, LINES), k) for k in range(2))
        above = exact((over < down).astype(jnp.float32), totals)
        table["code"] = (row * STRIDE + col).astype(jnp.float32)
        table["spot"] = jnp.where(match, left + above, -1.0)
        table["count"] = jnp.sum(totals, axis=0, keepdims=True)
        table["found"] = jnp.zeros((MOST, WIDE), jnp.float32)

    def do_find(begin):
        spots = lax.broadcasted_iota(jnp.int32, (MOST, WIDE), 0).astype(jnp.float32)
        for k in range(begin, begin + LINES // steps):
            row = slice(k, k + 1)
            table["found"] += jnp.where(table["spot"][row] == spots, table["code"][row], 0.0)

    def do_items():
        items = lax.dot_general(
            jnp.ones((8, WIDE), jnp.float32),
            table["found"],
            (((1,), (1,)), ((), ())),
            preferred_element_type=jnp.float32,
            precision=lax.Precision.HIGHEST,
        )
        many = jnp.concatenate([table["count"]] * (MOST // WIDE), axis=1)
        spot = lax.broadcasted_iota(jnp.int32, (8, MOST), 1).astype(jnp.float32)
        items = jnp.where(spot < many, items, float(NONE))
        at = lax.broadcasted_iota(jnp.int32, (8, MOST), 0)
        items_ref[...] = jnp.where(at == 0, items, many).astype(jnp.int32)

    work = [do_x_squares]
    work += [functools.partial(do_y_squares, k) for k in range(0, HALF, 8)]
    work += [do_bias, do_table]
    work += [functools.partial(do_find, k) for k in range(0, LINES, LINES // steps)]
    work += [do_items]
    for at, piece in enumerate(order):
        here = slot(piece)
        pltpu.make_async_copy(here, here, got.at[index[piece]]).wait()
        pass_on(piece)
        if piece[0][0] == "Y":
            pltpu.make_async_remote_copy(
                src_ref=here,
                dst_ref=here,
                send_sem=pair_sem.at[0],
                recv_sem=pair_sem.at[1],
                device_id=sibling,
                device_id_type=MESH,
            ).start()
        if at % 3 == 0 and work:
            work.pop(0)()
    while work:
        work.pop(0)()

    for copy in keeps:
        copy.wait()
    most = x_all.at[pl.ds(0, LINES - 1)]
    pltpu.make_async_copy(most, most, x_send).wait()
    most = y_all.at[pl.ds(0, NX - 1), :, pl.ds(0, Y_LANES)]
    for semaphore in (y_send, pair_sem.at[0], pair_sem.at[1]):
        pltpu.make_async_copy(most, most, semaphore).wait()
    most = bias_all.at[pl.ds(0, NX * NC - 1)]
    for side in range(2):
        pltpu.make_async_copy(most, most, bias_sem.at[side]).wait()


def gather(x_src, y_tgt, g_rows, owners, locals_, lives):
    count = len(gather_plan()[1])
    dma = pltpu.SemaphoreType.DMA
    hbm = pl.BlockSpec(memory_space=pltpu.HBM)
    return pl.pallas_call(
        gather_kernel,
        out_shape=(
            pltpu.VMEM((LINES, DIM, X_LANES), jnp.bfloat16),
            pltpu.VMEM((NX, DIM, NC * Y_LANES), jnp.bfloat16),
            jax.ShapeDtypeStruct((NX * NC, HALF, BLK), jnp.float32),
            jax.ShapeDtypeStruct((HALF_RB + HALF, BLK), jnp.float32),
            jax.ShapeDtypeStruct((8, MOST), jnp.int32),
        ),
        in_specs=[hbm, hbm, VMEM, VMEM, VMEM, SMEM],
        out_specs=(VMEM, VMEM, VMEM, VMEM, VMEM),
        scratch_shapes=[
            pltpu.VMEM((LINES * NC, 1, WIDE), jnp.int32),
            pltpu.VMEM((DIM, X_LANES), jnp.bfloat16),
            pltpu.VMEM((DIM, Y_LANES), jnp.bfloat16),
            dma((2,)),
            dma((2,)),
            dma((2,)),
            dma((2,)),
            dma,
            dma,
            dma((2,)),
            dma((count,)),
        ],
        compiler_params=pltpu.CompilerParams(
            collective_id=0, has_side_effects=True, vmem_limit_bytes=26 * 1024 * 1024
        ),
        name="gather",
    )(x_src, y_tgt, g_rows, owners, locals_, lives)


def potential(logit2):
    logit = logit2 * LN2
    top = jnp.maximum(logit, 0.0)
    return -EPSILON * (top + jnp.log(jnp.exp(-top) + jnp.exp(logit - top)))


def merged(parts):
    top = functools.reduce(jnp.maximum, parts)
    return top + jnp.log2(sum(jnp.exp2(part - top) for part in parts))


def exchange_kernel(
    part_ref, w_ref, squares_ref, f_ref, bias_ref, parts, part_sem, bias_sem, f_sem
):
    x, z, y, c = place()
    group = LINES
    me = z * NY + y

    def peer(k):
        other = lax.rem(me + k, group)
        return other, (x, other // NY, other % NY, c)

    barrier = pltpu.get_barrier_semaphore()

    def greet(k, carry):
        pl.semaphore_signal(barrier, inc=1, device_id=peer(k)[1], device_id_type=MESH)
        return carry

    sibling = (x, z, y, 1 - c)
    pl.semaphore_signal(barrier, inc=1, device_id=sibling, device_id_type=MESH)
    lax.fori_loop(1, group, greet, 0)
    pl.semaphore_wait(barrier, group)

    def send_part(k, carry):
        other, device = peer(k)
        pltpu.make_async_remote_copy(
            src_ref=part_ref.at[other],
            dst_ref=parts.at[me],
            send_sem=part_sem.at[0],
            recv_sem=part_sem.at[1],
            device_id=device,
            device_id_type=MESH,
        ).start()
        return carry

    lax.fori_loop(1, group, send_part, 0)
    parts[me] = part_ref[me]
    others = parts.at[pl.ds(0, group - 1)]
    pltpu.make_async_copy(others, others, part_sem.at[1]).wait()
    squares = squares_ref[...]
    f_half = potential(merged([parts[k] for k in range(group)]) - PER2 * squares)
    mine = pl.ds(pl.multiple_of(c * HALF_RB, HALF_RB), HALF_RB)
    f_ref[mine, :] = f_half
    bias_ref[me] = OFFSET * f_half + (EPSILON * OFFSET) * w_ref[mine, :] - squares

    def send_bias(k, carry):
        pltpu.make_async_remote_copy(
            src_ref=bias_ref.at[me],
            dst_ref=bias_ref.at[me],
            send_sem=bias_sem.at[0],
            recv_sem=bias_sem.at[1],
            device_id=peer(k)[1],
            device_id_type=MESH,
        ).start()
        return carry

    lax.fori_loop(1, group, send_bias, 0)
    over = pltpu.make_async_remote_copy(
        src_ref=f_ref.at[mine, :],
        dst_ref=f_ref.at[mine, :],
        send_sem=f_sem.at[0],
        recv_sem=f_sem.at[1],
        device_id=sibling,
        device_id_type=MESH,
    )
    over.start()
    pltpu.make_async_copy(others, others, part_sem.at[0]).wait()
    others = bias_ref.at[pl.ds(0, group - 1)]
    for side in range(2):
        pltpu.make_async_copy(others, others, bias_sem.at[side]).wait()
    over.wait()


def exchange(partial, w_rows, squares):
    dma = pltpu.SemaphoreType.DMA
    group = LINES
    return pl.pallas_call(
        exchange_kernel,
        out_shape=(
            jax.ShapeDtypeStruct((RB_DEV, BLK), jnp.float32),
            jax.ShapeDtypeStruct((group, HALF_RB, BLK), jnp.float32),
        ),
        in_specs=[VMEM, VMEM, VMEM],
        out_specs=(VMEM, VMEM),
        scratch_shapes=[
            pltpu.VMEM((group, HALF_RB, BLK), jnp.float32),
            dma((2,)),
            dma((2,)),
            dma((2,)),
        ],
        compiler_params=pltpu.CompilerParams(
            collective_id=1, has_side_effects=True, vmem_limit_bytes=16 * 1024 * 1024
        ),
        name="exchange",
    )(partial, w_rows, squares)


def finish_kernel(part_ref, squares_ref, g_ref, parts, part_sem, g_sem):
    x, z, y, c = place()
    barrier = pltpu.get_barrier_semaphore()
    group = NX * NC
    me = x * NC + c
    peers = [lax.rem(me + k, group) for k in range(1, group)]
    sibling = (x, z, y, 1 - c)
    for other in peers:
        pl.semaphore_signal(
            barrier, inc=1, device_id=(other // NC, z, y, other % NC), device_id_type=MESH
        )
    pl.semaphore_wait(barrier, group - 1)
    for other in peers:
        pltpu.make_async_remote_copy(
            src_ref=part_ref.at[other],
            dst_ref=parts.at[me],
            send_sem=part_sem.at[0],
            recv_sem=part_sem.at[1],
            device_id=(other // NC, z, y, other % NC),
            device_id_type=MESH,
        ).start()
    parts[me] = part_ref[me]
    others = parts.at[pl.ds(0, group - 1)]
    pltpu.make_async_copy(others, others, part_sem.at[1]).wait()
    g_half = potential(merged([parts[k] for k in range(group)]) - PER2 * squares_ref[...])
    mine = pl.ds(pl.multiple_of(c * HALF, HALF), HALF)
    g_ref[mine, :] = g_half
    over = pltpu.make_async_remote_copy(
        src_ref=g_ref.at[mine, :],
        dst_ref=g_ref.at[mine, :],
        send_sem=g_sem.at[0],
        recv_sem=g_sem.at[1],
        device_id=sibling,
        device_id_type=MESH,
    )
    over.start()
    pltpu.make_async_copy(others, others, part_sem.at[0]).wait()
    over.wait()


def finish(partial, squares):
    dma = pltpu.SemaphoreType.DMA
    return pl.pallas_call(
        finish_kernel,
        out_shape=jax.ShapeDtypeStruct((TB_DEV, BLK), jnp.float32),
        in_specs=[VMEM, VMEM],
        out_specs=VMEM,
        scratch_shapes=[pltpu.VMEM((NX * NC, HALF, BLK), jnp.float32), dma((2,)), dma((2,))],
        compiler_params=pltpu.CompilerParams(
            collective_id=2, has_side_effects=True, vmem_limit_bytes=16 * 1024 * 1024
        ),
        name="finish",
    )(partial, squares)


def on_device(x_src, w_src, y_tgt, g_in, support_owner, support_local, live_count):
    x_all, y_all, bias_all, squares, items = gather(
        x_src, y_tgt, g_in.reshape(TB_DEV, BLK), support_owner, support_local, live_count
    )
    partial = local_call(
        row_kernel, ROWS, [pltpu.VMEM((NX * NC + 1, ROWS, BLK), jnp.float32)], "rows"
    )(items, x_all, y_all, bias_all.reshape(NONE, BLK))
    f_new, bias_rows = exchange(
        partial.reshape(LINES, HALF_RB, BLK), w_src.reshape(RB_DEV, BLK), squares[:HALF_RB]
    )
    col = local_call(
        column_kernel,
        NONE,
        [pltpu.VMEM((NONE + 8, BLK), jnp.float32), pltpu.VMEM((NONE + 8, BLK), jnp.float32)],
        "columns",
    )(items, x_all, y_all, bias_rows.reshape(ROWS, BLK))
    g_new = finish(col.reshape(NX * NC, HALF, BLK), squares[HALF_RB:])
    return f_new.reshape(RB_DEV * BLK), g_new.reshape(TB_DEV * BLK)


def solution(mesh):
    fine = Mesh(mesh.devices.reshape(NX, NZ, NY, NC), ("x", "z", "y", "core"))
    src = ("x", "z", "y")
    placed = (
        P(None, src),
        P(src),
        P(None, src),
        P(src),
        P("core", src, None),
        P("core", src, None),
        P("core", src),
    )
    return jax.shard_map(
        on_device, mesh=fine, in_specs=placed, out_specs=(P(src), P(src)), check_vma=False
    )
```

time: 193 us -> 133 us (0.69)
  the two profiles are of different devices: /device:TPU:9 before, /device:TPU:1 now
where the time goes in v3:
time: 133 us; the launch traced here: 132 us
  Pallas kernels  124 us (93%)
  local copies, waits for them, and re-layouts  7.58 us (6%)
    pallas_call x1, Pallas kernels, gather(): pl.pallas_call(gather_kernel, out_shape=(pltpu.VMEM((LINES, DIM, X_LANES)...  63.6 us
    pallas_call x1, Pallas kernels, exchange(): pl.pallas_call(exchange_kernel, out_shape=(jax.ShapeDtypeStruct((RB_DEV,...  22.1 us
    pallas_call x1, Pallas kernels, finish(): pl.pallas_call(finish_kernel, out_shape=jax.ShapeDtypeStruct((TB_DEV, BLK...  17.6 us
    pallas_call x1, Pallas kernels, on_device(): local_call(row_kernel, ROWS, [pltpu.VMEM((NX * NC + 1, ROWS, BLK), jnp.fl...  10.3 us
    pallas_call x1, Pallas kernels, on_device(): local_call(column_kernel, NONE, [pltpu.VMEM((NONE + 8, BLK), jnp.float32)...  10.2 us
    unnamed x10, local copies, waits for them, and re-layouts  6.08 us

profile of v3, /device:TPU:1, one launch (start us, length us, event | category | flops | bytes accessed | tf_op | source)
XLA Modules:
  0.0 132.0 jit_solution(15827725629742847558)
XLA Ops:
  0.6 0.8 copy.9.owner_ref
  1.4 0.8 copy.10.local_ref
  2.1 0.7 reshape.31.w_ref
  2.9 0.8 reshape.28.g_ref
  3.6 0.0 copy-start
  3.7 1.6 %copy-done = bf16[64,16384]{1,0:T(8,128)(2,1)S(1)} copy-done((bf16[64,16384]{1,0:T(8,128)(2,1)S(1)}, bf16[64,16384]{1,0:T(8,128)(2,1)}, u32[]{:S(2)}) %copy-start) | copy-done | bytes 2097176
  5.2 0.0 copy-start.1
  5.2 1.0 copy-done.1
  6.3 0.0 copy-start.2
  6.3 0.7 copy-done.2
  6.9 63.6 %gather.1 = (bf16[32,64,2048]{2,1,0:T(8,128)(2,1)S(1)}, bf16[4,64,16384]{2,1,0:T(8,128)(2,1)S(1)}, f32[8,32,256]{2,1,0:T(8,128)S(1)}, f32[40,256]{1,0:T(8,128)S(1)}, s32[8,512]{1,0:T(8,128)S(1)}) custom-call(bf16[64,4096]{1,0:T(8,128)(2,1)S(1)} %copy-done.1, bf16[64,16384]{1,0:T(8,128)(2,1)S(1)} %copy-done, bf16[64,256]{1,0:T(8,128)(2,1)S(1)} %reshape.28.g_ref, ...), custom_call_target="tpu_custom_call" | custom-call | tf_op jit(solution)/shard_map/gather/pallas_call | solution.py:446
  70.5 10.3 %rows.1 = f32[256,256]{1,0:T(8,128)S(1)} custom-call(s32[8,512]{1,0:T(8,128)S(1)} %get-tuple-element.9.items_ref, bf16[32,64,2048]{2,1,0:T(8,128)(2,1)S(1)} %get-tuple-element.10.x_ref, bf16[4,64,16384]{2,1,0:T(8,128)(2,1)S(1)} %get-tuple-element.11.y_ref, f32[256,256]{1,0:T(8,128)S(1)} %bitcast.11), custom_call_target="tpu_custom_call" | custom-call | tf_op jit(solution)/shard_map/rows/pallas_call | solution.py:643
  80.8 22.1 %exchange.1 = (f32[16,256]{1,0:T(8,128)S(1)}, f32[32,8,256]{2,1,0:T(8,128)S(1)}) custom-call(f32[32,8,256]{2,1,0:T(8,128)S(1)} %bitcast.8, f32[16,256]{1,0:T(8,128)S(1)} %reshape.31.w_ref, f32[8,256]{1,0:T(8,128)S(1)} %slice.6.squares_ref), custom_call_target="tpu_custom_call" | custom-call | tf_op jit(solution)/shard_map/exchange/pallas_call | solution.py:563
  102.9 0.6 copy.11
  103.6 10.2 %columns.1 = f32[256,256]{1,0:T(8,128)S(1)} custom-call(s32[8,512]{1,0:T(8,128)S(1)} %get-tuple-element.9.items_ref, bf16[32,64,2048]{2,1,0:T(8,128)(2,1)S(1)} %get-tuple-element.10.x_ref, bf16[4,64,16384]{2,1,0:T(8,128)(2,1)S(1)} %get-tuple-element.11.y_ref, f32[256,256]{1,0:T(8,128)S(1)} %bitcast.10), custom_call_target="tpu_custom_call" | custom-call | tf_op jit(solution)/shard_map/columns/pallas_call | solution.py:649
  113.8 17.6 %finish.1 = f32[64,256]{1,0:T(8,128)S(1)} custom-call(f32[8,32,256]{2,1,0:T(8,128)S(1)} %bitcast.9, f32[32,256]{1,0:T(8,128)S(1)} %slice.7.squares_ref), custom_call_target="tpu_custom_call" | custom-call | tf_op jit(solution)/shard_map/finish/pallas_call | solution.py:626
  131.4 0.7 copy.12
  (2 shorter events, 0.0 us)
Async XLA Ops:
  3.6 1.6 %copy-start = (bf16[64,16384]{1,0:T(8,128)(2,1)S(1)}, bf16[64,16384]{1,0:T(8,128)(2,1)}, u32[]{:S(2)}) copy-start(bf16[64,16384]{1,0:T(8,128)(2,1)} %y_ref.1) | copy-start | bytes 6291460
  5.2 1.0 copy-start.1
  6.3 0.7 copy-start.2

commit v4 on v3

v4 whole, which is shorter than its diff:
```python
import functools
import heapq

import jax
import jax.numpy as jnp
import numpy as np
from jax import lax
from jax.experimental import pallas as pl
from jax.experimental.pallas import tpu as pltpu
from jax.sharding import Mesh, PartitionSpec as P

DIM = 64
BLK = 256
KH = 8
RB_DEV = 16
TB_DEV = 64
HALF = TB_DEV // 2

EPSILON = 0.1
EMPTY = -1e30
PER = 2.0 / (DIM * EPSILON)
PER2 = PER * float(np.log2(np.e))
OFFSET = DIM / 2.0
LN2 = float(np.log(2.0))
AUG = 16

MESH = pl.DeviceIdType.MESH
NX, NZ, NY, NC = 4, 8, 4, 2
LINES = NZ * NY
HALF_RB = RB_DEV // 2
ROWS = LINES * HALF_RB
NONE = NX * TB_DEV
STRIDE = 2 * NONE
MOST = LINES * 2 * NX * NC
WIDE = RB_DEV * KH
X_LANES = HALF_RB * BLK
Y_LANES = HALF * BLK
UNROLL = 16
SAFE = 100.0


def extra_rows(row, at_left):
    high = row.astype(jnp.bfloat16).astype(jnp.float32)
    middle = (row - high).astype(jnp.bfloat16).astype(jnp.float32)
    low = row - high - middle
    at = lax.broadcasted_iota(jnp.int32, (AUG, BLK), 0)
    base = 0 if at_left else 3
    ones = jnp.where(at < 6, 1.0, 0.0)
    parts = jnp.where(at == base + 1, middle, jnp.where(at == base + 2, low, ones))
    return jnp.where(at == base, high, parts).astype(jnp.bfloat16)


def squares_of(tile):
    return 0.5 * jnp.sum(jnp.square(tile.astype(jnp.float32)), axis=0, keepdims=True)


def log2_mass(mass):
    return jnp.maximum(jnp.log2(mass), EMPTY)


def tile_logits(left, right):
    return lax.dot_general(
        left, right, (((0,), (0,)), ((), ())), preferred_element_type=jnp.float32
    )


def peak_and_mass(tile):
    peak = jnp.max(tile, axis=0, keepdims=True)
    mass = jnp.sum(jnp.exp2((tile - peak) * PER2), axis=0, keepdims=True)
    return peak, mass


def lane_block(index):
    return pl.ds(pl.multiple_of(index * BLK, BLK), BLK)


def x_tile(x_ref, block):
    return x_ref[block // HALF_RB, :, lane_block(block % HALF_RB)]


def y_tile(y_ref, block):
    return y_ref[block // TB_DEV, :, lane_block(block % TB_DEV)]


def for_pairs(items_ref, visit):
    def step(group, carry):
        for k in range(UNROLL):
            code = items_ref[0, group * UNROLL + k]
            visit(code // STRIDE, code % STRIDE)
        return carry

    lax.fori_loop(0, (items_ref[1, 0] + UNROLL - 1) // UNROLL, step, 0)


def plain_mass(tile):
    return jnp.sum(jnp.exp2(tile * PER2), axis=0, keepdims=True)


def one_of(col):
    return col // HALF, pl.ds(col % HALF, 1)


def row_kernel(items_ref, x_ref, y_ref, info_ref, out_ref, slots, bias):
    bias[...] = info_ref[:, 0] - info_ref[:, 1]
    safe = jnp.max(info_ref[:, 0]) * PER2 <= SAFE

    def logits(row, col):
        half, at = one_of(col % NONE)
        left = jnp.concatenate(
            [y_tile(y_ref, col % NONE), extra_rows(bias[half, at, :], True)], axis=0
        )
        tile = x_tile(x_ref, row)
        right = jnp.concatenate([tile, extra_rows(-squares_of(tile), False)], axis=0)
        return tile_logits(left, right)

    @pl.when(safe)
    def _():
        slots[...] = jnp.zeros(slots.shape, jnp.float32)

        def visit(row, col):
            slots[col // HALF, pl.ds(row, 1), :] = plain_mass(logits(row, col))

        for_pairs(items_ref, visit)
        out_ref[...] = log2_mass(sum(slots[k] for k in range(NC * NX)))

    @pl.when(jnp.logical_not(safe))
    def _():
        slots[...] = jnp.full(slots.shape, EMPTY, jnp.float32)

        def visit(row, col):
            peak, mass = peak_and_mass(logits(row, col))
            slots[col // HALF, pl.ds(row, 1), :] = peak * PER2 + jnp.log2(mass)

        for_pairs(items_ref, visit)
        out_ref[...] = merged([slots[k] for k in range(NC * NX)])


def column_kernel(
    items_ref, x_ref, y_ref, info_ref, offset_ref, out_ref, peaks, masses
):
    masses[...] = jnp.zeros(masses.shape, jnp.float32)
    safe = jnp.max(offset_ref[...]) * PER2 <= SAFE

    def logits(row, col):
        half, at = one_of(col % NONE)
        tile = x_tile(x_ref, row)
        bias = offset_ref[pl.ds(row, 1), :] - squares_of(tile)
        left = jnp.concatenate([tile, extra_rows(bias, True)], axis=0)
        square = info_ref[half, 1, at, :]
        right = jnp.concatenate(
            [y_tile(y_ref, col % NONE), extra_rows(-square, False)], axis=0
        )
        return tile_logits(left, right)

    @pl.when(safe)
    def _():
        def visit(row, col):
            masses[pl.ds(col, 1), :] += plain_mass(logits(row, col))

        for_pairs(items_ref, visit)
        out_ref[...] = log2_mass(masses[0:NONE, :])

    @pl.when(jnp.logical_not(safe))
    def _():
        peaks[...] = jnp.full(peaks.shape, EMPTY, jnp.float32)

        def visit(row, col):
            peak, mass = peak_and_mass(logits(row, col))
            old = peaks[pl.ds(col, 1), :]
            new = jnp.maximum(old, peak)
            peaks[pl.ds(col, 1), :] = new
            masses[pl.ds(col, 1), :] = masses[pl.ds(col, 1), :] * jnp.exp2(
                (old - new) * PER2
            ) + mass * jnp.exp2((peak - new) * PER2)

        for_pairs(items_ref, visit)
        out_ref[...] = jnp.maximum(
            peaks[0:NONE, :] * PER2 + log2_mass(masses[0:NONE, :]), EMPTY
        )


SMEM = pl.BlockSpec(memory_space=pltpu.SMEM)
VMEM = pl.BlockSpec(memory_space=pltpu.VMEM)


def local_call(body, arrays, out_rows, scratch, name):
    return pl.pallas_call(
        body,
        out_shape=jax.ShapeDtypeStruct((out_rows, BLK), jnp.float32),
        in_specs=[SMEM] + [VMEM] * arrays,
        out_specs=VMEM,
        scratch_shapes=scratch,
        compiler_params=pltpu.CompilerParams(vmem_limit_bytes=26 * 1024 * 1024),
        name=name,
    )


FIRST = ("Bl", "Bh", "A")
PARTS = {"A": (0, 3, 1), "Bl": (3, 2, -1), "Bh": (5, 3, 1)}
Y_CHUNKS = 4
CHUNK = Y_LANES // Y_CHUNKS


def anywhere():
    return pl.BlockSpec(memory_space=pl.ANY)


def place():
    return tuple(lax.axis_index(axis) for axis in ("x", "z", "y", "core"))


def moved(size, offset):
    longest = {8: 4, 4: 2}[size]
    shortest = size - 1 - longest
    out = []
    if -longest < offset <= 0:
        out.append((1, offset - 1))
    if 0 <= offset < shortest:
        out.append((-1, offset + 1))
    return out


def way(kind):
    if kind in PARTS:
        return PARTS[kind][2]
    return -1 if kind[0] == "Y" and int(kind[1:]) % 2 else 1


def onward(piece):
    kind, a, b = piece
    if kind[0] == "A":
        found = [("z", d, (kind, n, b)) for d, n in moved(NZ, a)]
        if a == 0:
            found += [("y", d, (kind, 0, n)) for d, n in moved(NY, b)]
    elif kind[0] in "BC":
        found = [("z", d, (kind, n, 0)) for d, n in moved(NZ, a)] if b == 0 else []
        found += [("y", d, (kind, a, n)) for d, n in moved(NY, b)]
    else:
        found = [("x", d, (kind, n, 0)) for d, n in moved(NX, a)]
    return found


def gather_plan():
    took = {kind: part[1] * BLK for kind, part in PARTS.items()} | {"C": 4}
    kinds = [f"Y{k}" for k in range(Y_CHUNKS)]
    took |= {kind: CHUNK for kind in kinds}
    first = [(kind, 0, 0) for kind in ["C", *FIRST, *kinds]]
    free, waiting, order = {}, [], []

    def send(now, piece):
        for axis, direction, seen in onward(piece):
            link = (axis, direction * way(piece[0]))
            end = max(now, free.get(link, 0.0)) + took[piece[0]]
            free[link] = end
            heapq.heappush(waiting, (end + 384.0, seen))

    for piece in first:
        send(0.0, piece)
    while waiting:
        now, piece = heapq.heappop(waiting)
        order.append(piece)
        send(now, piece)
    return first, order


def gather_kernel(
    x_ref, y_ref, g_ref, owner_ref, local_ref, live_ref,
    x_all, y_all, info_all, items_ref,
    codes, y_own, info_sem, code_sem, code_send, own_sem, keep_sem, x_send, y_send, pair_sem, got,
):
    x, z, y, c = place()
    turn = 1 - 2 * c
    line = z * NY + y
    first, order = gather_plan()
    index = {piece: k for k, piece in enumerate(order)}

    barrier = pltpu.get_barrier_semaphore()
    sibling = (x, z, y, 1 - c)

    line_peers = [(lax.rem(x + k, NX), z, y, core) for k in range(1, NX) for core in range(NC)]
    near = [(x, lax.rem(z + k, NZ), y, c) for k in (1, NZ - 1)]
    near += [(x, z, lax.rem(y + k, NY), c) for k in (1, NY - 1)]
    near += [sibling] + line_peers
    for device in near:
        pl.semaphore_signal(barrier, inc=1, device_id=device, device_id_type=MESH)

    x_mine = pl.multiple_of(c * X_LANES, X_LANES)
    y_mine = pl.multiple_of(c * Y_LANES, Y_LANES)
    own = pltpu.make_async_copy(y_ref.at[:, pl.ds(y_mine, Y_LANES)], y_own, own_sem)
    keeps = [
        pltpu.make_async_copy(
            x_ref.at[:, pl.ds(x_mine, X_LANES)], x_all.at[line], keep_sem.at[0]
        ),
        pltpu.make_async_copy(y_ref, y_all.at[x], keep_sem.at[1]),
    ]
    for copy in [own] + keeps:
        copy.start()

    exact = functools.partial(
        jnp.dot, preferred_element_type=jnp.float32, precision=lax.Precision.HIGHEST
    )
    slot_at = lax.broadcasted_iota(jnp.int32, (KH, RB_DEV), 0)
    listed = owner_ref[0] * HALF + local_ref[0]
    listed = jnp.where(slot_at < live_ref[...], listed, -1).astype(jnp.float32)
    down, over = (lax.broadcasted_iota(jnp.int32, (RB_DEV, WIDE), k) for k in range(2))
    spread = exact(listed, (over // KH == down).astype(jnp.float32))
    down, over = (lax.broadcasted_iota(jnp.int32, (KH, WIDE), k) for k in range(2))
    codes[c, line] = jnp.sum(
        jnp.where(over % KH == down, spread, 0.0), axis=0, keepdims=True
    ).astype(jnp.int32)
    pl.semaphore_wait(barrier, len(near))

    def lanes_of(kind):
        if kind in PARTS:
            return PARTS[kind][0] * BLK, PARTS[kind][1] * BLK
        return int(kind[1:]) * CHUNK, CHUNK

    def slot(piece):
        kind, a, b = piece
        ahead = turn * way(kind)
        origin = lax.rem(z + ahead * a + NZ, NZ) * NY + lax.rem(y + ahead * b + NY, NY)
        if kind == "C":
            return codes.at[c, origin]
        begin, width = lanes_of(kind)
        if kind[0] == "Y":
            there = pl.ds(pl.multiple_of(y_mine + begin, BLK), width)
            return y_all.at[lax.rem(x + ahead * a + NX, NX), :, there]
        return x_all.at[origin, :, pl.ds(begin, width)]

    def source(piece):
        kind, a, b = piece
        if a or b or kind == "C":
            return slot(piece)
        begin, width = lanes_of(kind)
        if kind[0] == "Y":
            return y_ref.at[:, pl.ds(pl.multiple_of(y_mine + begin, BLK), width)]
        return x_ref.at[:, pl.ds(pl.multiple_of(x_mine + begin, BLK), width)]

    def neighbour(axis, direction):
        step = turn * direction
        return (
            lax.rem(x + step + NX, NX) if axis == "x" else x,
            lax.rem(z + step + NZ, NZ) if axis == "z" else z,
            lax.rem(y + step + NY, NY) if axis == "y" else y,
            c,
        )

    def pass_on(piece):
        for axis, direction, seen in onward(piece):
            pltpu.make_async_remote_copy(
                src_ref=source(piece),
                dst_ref=slot(piece),
                send_sem={"Y": y_send, "C": code_send}.get(piece[0][0], x_send),
                recv_sem=got.at[index[seen]],
                device_id=neighbour(axis, direction * way(piece[0])),
                device_id_type=MESH,
            ).start()

    for piece in first:
        pass_on(piece)

    info = info_all.at[x * NC + c]

    def do_y_squares(begin):
        if begin == 0:
            own.wait()
        for k in range(begin, begin + 8):
            info[1, k : k + 1, :] = squares_of(y_own[:, k * BLK : (k + 1) * BLK])

    def do_info():
        g_half = jnp.where(c == 0, g_ref[:HALF, :], g_ref[HALF:, :])
        info[0] = OFFSET * g_half.astype(jnp.float32)
        for device in line_peers + [sibling]:
            pltpu.make_async_remote_copy(
                src_ref=info,
                dst_ref=info,
                send_sem=info_sem.at[0],
                recv_sem=info_sem.at[1],
                device_id=device,
                device_id_type=MESH,
            ).start()

    def over_codes():
        return pltpu.make_async_remote_copy(
            src_ref=codes.at[c],
            dst_ref=codes.at[c],
            send_sem=code_sem.at[0],
            recv_sem=code_sem.at[1],
            device_id=sibling,
            device_id_type=MESH,
        )

    table = {}
    steps = 4

    def do_table():
        over_codes().wait()
        halves = [codes[k].reshape(LINES, WIDE) for k in range(NC)]
        lane = lax.broadcasted_iota(jnp.int32, (LINES, WIDE), 1)
        turned = [pltpu.roll(part, WIDE // 2, 1) for part in halves]
        even = jnp.where(lane < WIDE // 2, halves[0], turned[1])
        odd = jnp.where(lane < WIDE // 2, turned[0], halves[1])
        entry = jnp.where(c == 0, even, odd)
        owner = entry // HALF
        match = (entry >= 0) & (owner % LINES == line)
        row = (
            lax.broadcasted_iota(jnp.int32, entry.shape, 0) * HALF_RB
            + lane % (WIDE // 2) // KH
        )
        col = owner // LINES * TB_DEV + lane // (WIDE // 2) * HALF + entry % HALF
        hits = match.astype(jnp.float32)
        down, over = (lax.broadcasted_iota(jnp.int32, (WIDE, WIDE), k) for k in range(2))
        left = exact(hits, (down < over).astype(jnp.float32))
        totals = exact(hits, jnp.ones((WIDE, WIDE), jnp.float32))
        down, over = (lax.broadcasted_iota(jnp.int32, (LINES, LINES), k) for k in range(2))
        above = exact((over < down).astype(jnp.float32), totals)
        table["code"] = (row * STRIDE + col).astype(jnp.float32)
        table["spot"] = jnp.where(match, left + above, -1.0)
        table["count"] = jnp.sum(totals, axis=0, keepdims=True)
        table["found"] = jnp.zeros((MOST, WIDE), jnp.float32)

    def do_find(begin):
        spots = lax.broadcasted_iota(jnp.int32, (MOST, WIDE), 0).astype(jnp.float32)
        for k in range(begin, begin + LINES // steps):
            row = slice(k, k + 1)
            table["found"] += jnp.where(table["spot"][row] == spots, table["code"][row], 0.0)

    def do_items():
        items = lax.dot_general(
            jnp.ones((8, WIDE), jnp.float32),
            table["found"],
            (((1,), (1,)), ((), ())),
            preferred_element_type=jnp.float32,
            precision=lax.Precision.HIGHEST,
        )
        many = jnp.concatenate([table["count"]] * (MOST // WIDE), axis=1)
        spot = lax.broadcasted_iota(jnp.int32, (8, MOST), 1).astype(jnp.float32)
        items = jnp.where(spot < many, items, float(NONE))
        at = lax.broadcasted_iota(jnp.int32, (8, MOST), 0)
        items_ref[...] = jnp.where(at == 0, items, many).astype(jnp.int32)

    early = [functools.partial(do_y_squares, k) for k in range(0, HALF, 8)]
    early += [do_info]
    late = [do_table]
    late += [functools.partial(do_find, k) for k in range(0, LINES, LINES // steps)]
    late += [do_items]
    codes_left, between = LINES - 1, 0
    for piece in order:
        here = slot(piece)
        pltpu.make_async_copy(here, here, got.at[index[piece]]).wait()
        pass_on(piece)
        if piece[0] == "C":
            codes_left -= 1
            if codes_left == 0:
                over_codes().start()
            continue
        if piece[0][0] == "Y":
            pltpu.make_async_remote_copy(
                src_ref=here,
                dst_ref=here,
                send_sem=pair_sem.at[0],
                recv_sem=pair_sem.at[1],
                device_id=sibling,
                device_id_type=MESH,
            ).start()
        between += 1
        if between % 3 == 0:
            if early:
                early.pop(0)()
            elif late and codes_left == 0:
                late.pop(0)()
    for task in early + late:
        task()

    for copy in keeps:
        copy.wait()
    most = x_all.at[pl.ds(0, LINES - 1)]
    pltpu.make_async_copy(most, most, x_send).wait()
    most = y_all.at[pl.ds(0, NX - 1), :, pl.ds(0, Y_LANES)]
    for semaphore in (y_send, pair_sem.at[0], pair_sem.at[1]):
        pltpu.make_async_copy(most, most, semaphore).wait()
    most = info_all.at[pl.ds(0, NX * NC - 1)]
    for side in range(2):
        pltpu.make_async_copy(most, most, info_sem.at[side]).wait()
    most = codes.at[0, pl.ds(0, LINES - 1)]
    pltpu.make_async_copy(most, most, code_send).wait()


def gather(x_src, y_tgt, g_rows, owners, locals_, lives):
    count = len(gather_plan()[1])
    dma = pltpu.SemaphoreType.DMA
    hbm = pl.BlockSpec(memory_space=pltpu.HBM)
    return pl.pallas_call(
        gather_kernel,
        out_shape=(
            pltpu.VMEM((LINES, DIM, X_LANES), jnp.bfloat16),
            pltpu.VMEM((NX, DIM, NC * Y_LANES), jnp.bfloat16),
            jax.ShapeDtypeStruct((NX * NC, 2, HALF, BLK), jnp.float32),
            jax.ShapeDtypeStruct((8, MOST), jnp.int32),
        ),
        in_specs=[hbm, hbm, VMEM, VMEM, VMEM, VMEM],
        out_specs=(VMEM, VMEM, VMEM, VMEM),
        scratch_shapes=[
            pltpu.VMEM((NC, LINES, 1, WIDE), jnp.int32),
            pltpu.VMEM((DIM, Y_LANES), jnp.bfloat16),
            dma((2,)),
            dma((2,)),
            dma,
            dma,
            dma((2,)),
            dma,
            dma,
            dma((2,)),
            dma((count,)),
        ],
        compiler_params=pltpu.CompilerParams(
            collective_id=0, has_side_effects=True, vmem_limit_bytes=26 * 1024 * 1024
        ),
        name="gather",
    )(x_src, y_tgt, g_rows, owners, locals_, lives)


def potential(logit2):
    logit = logit2 * LN2
    top = jnp.maximum(logit, 0.0)
    return -EPSILON * (top + jnp.log(jnp.exp(-top) + jnp.exp(logit - top)))


def merged(parts):
    top = functools.reduce(jnp.maximum, parts)
    return top + jnp.log2(sum(jnp.exp2(part - top) for part in parts))


def exchange_kernel(
    part_ref, w_ref, f_ref, bias_ref, parts, part_sem, bias_sem, f_sem
):
    x, z, y, c = place()
    group = LINES
    me = z * NY + y

    def peer(k):
        other = lax.rem(me + k, group)
        return other, (x, other // NY, other % NY, c)

    barrier = pltpu.get_barrier_semaphore()

    def greet(k, carry):
        pl.semaphore_signal(barrier, inc=1, device_id=peer(k)[1], device_id_type=MESH)
        return carry

    sibling = (x, z, y, 1 - c)
    pl.semaphore_signal(barrier, inc=1, device_id=sibling, device_id_type=MESH)
    lax.fori_loop(1, group, greet, 0)
    pl.semaphore_wait(barrier, group)

    def send_part(k, carry):
        other, device = peer(k)
        pltpu.make_async_remote_copy(
            src_ref=part_ref.at[other],
            dst_ref=parts.at[me],
            send_sem=part_sem.at[0],
            recv_sem=part_sem.at[1],
            device_id=device,
            device_id_type=MESH,
        ).start()
        return carry

    lax.fori_loop(1, group, send_part, 0)
    parts[me] = part_ref[me]
    others = parts.at[pl.ds(0, group - 1)]
    pltpu.make_async_copy(others, others, part_sem.at[1]).wait()
    f_half = potential(merged([parts[k] for k in range(group)]))
    mine = pl.ds(pl.multiple_of(c * HALF_RB, HALF_RB), HALF_RB)
    f_ref[mine, :] = f_half
    bias_ref[me] = OFFSET * f_half + (EPSILON * OFFSET) * w_ref[mine, :]

    def send_bias(k, carry):
        pltpu.make_async_remote_copy(
            src_ref=bias_ref.at[me],
            dst_ref=bias_ref.at[me],
            send_sem=bias_sem.at[0],
            recv_sem=bias_sem.at[1],
            device_id=peer(k)[1],
            device_id_type=MESH,
        ).start()
        return carry

    lax.fori_loop(1, group, send_bias, 0)
    over = pltpu.make_async_remote_copy(
        src_ref=f_ref.at[mine, :],
        dst_ref=f_ref.at[mine, :],
        send_sem=f_sem.at[0],
        recv_sem=f_sem.at[1],
        device_id=sibling,
        device_id_type=MESH,
    )
    over.start()
    pltpu.make_async_copy(others, others, part_sem.at[0]).wait()
    others = bias_ref.at[pl.ds(0, group - 1)]
    for side in range(2):
        pltpu.make_async_copy(others, others, bias_sem.at[side]).wait()
    over.wait()


def exchange(partial, w_rows):
    dma = pltpu.SemaphoreType.DMA
    group = LINES
    return pl.pallas_call(
        exchange_kernel,
        out_shape=(
            jax.ShapeDtypeStruct((RB_DEV, BLK), jnp.float32),
            jax.ShapeDtypeStruct((group, HALF_RB, BLK), jnp.float32),
        ),
        in_specs=[VMEM, VMEM],
        out_specs=(VMEM, VMEM),
        scratch_shapes=[
            pltpu.VMEM((group, HALF_RB, BLK), jnp.float32),
            dma((2,)),
            dma((2,)),
            dma((2,)),
        ],
        compiler_params=pltpu.CompilerParams(
            collective_id=1, has_side_effects=True, vmem_limit_bytes=16 * 1024 * 1024
        ),
        name="exchange",
    )(partial, w_rows)


def finish_kernel(part_ref, g_ref, parts, part_sem, g_sem):
    x, z, y, c = place()
    barrier = pltpu.get_barrier_semaphore()
    group = NX * NC
    me = x * NC + c
    peers = [lax.rem(me + k, group) for k in range(1, group)]
    sibling = (x, z, y, 1 - c)
    for other in peers:
        pl.semaphore_signal(
            barrier, inc=1, device_id=(other // NC, z, y, other % NC), device_id_type=MESH
        )
    pl.semaphore_wait(barrier, group - 1)
    for other in peers:
        pltpu.make_async_remote_copy(
            src_ref=part_ref.at[other],
            dst_ref=parts.at[me],
            send_sem=part_sem.at[0],
            recv_sem=part_sem.at[1],
            device_id=(other // NC, z, y, other % NC),
            device_id_type=MESH,
        ).start()
    parts[me] = part_ref[me]
    others = parts.at[pl.ds(0, group - 1)]
    pltpu.make_async_copy(others, others, part_sem.at[1]).wait()
    g_half = potential(merged([parts[k] for k in range(group)]))
    mine = pl.ds(pl.multiple_of(c * HALF, HALF), HALF)
    g_ref[mine, :] = g_half
    over = pltpu.make_async_remote_copy(
        src_ref=g_ref.at[mine, :],
        dst_ref=g_ref.at[mine, :],
        send_sem=g_sem.at[0],
        recv_sem=g_sem.at[1],
        device_id=sibling,
        device_id_type=MESH,
    )
    over.start()
    pltpu.make_async_copy(others, others, part_sem.at[0]).wait()
    over.wait()


def finish(partial):
    dma = pltpu.SemaphoreType.DMA
    return pl.pallas_call(
        finish_kernel,
        out_shape=jax.ShapeDtypeStruct((TB_DEV, BLK), jnp.float32),
        in_specs=[VMEM],
        out_specs=VMEM,
        scratch_shapes=[pltpu.VMEM((NX * NC, HALF, BLK), jnp.float32), dma((2,)), dma((2,))],
        compiler_params=pltpu.CompilerParams(
            collective_id=2, has_side_effects=True, vmem_limit_bytes=16 * 1024 * 1024
        ),
        name="finish",
    )(partial)


def on_device(x_src, w_src, y_tgt, g_in, support_owner, support_local, live_count):
    f32 = jnp.float32
    x_all, y_all, info, items = gather(
        pltpu.with_memory_space_constraint(x_src, pltpu.HBM),
        pltpu.with_memory_space_constraint(y_tgt, pltpu.HBM),
        g_in.reshape(TB_DEV, BLK),
        jnp.swapaxes(support_owner, 1, 2),
        jnp.swapaxes(support_local, 1, 2),
        live_count,
    )
    shared = (items, x_all, y_all, info)
    scratch = [pltpu.VMEM((NX * NC + 1, ROWS, BLK), f32), pltpu.VMEM((NX * NC, HALF, BLK), f32)]
    partial = local_call(row_kernel, 3, ROWS, scratch, "rows")(*shared)
    f_new, offsets = exchange(
        partial.reshape(LINES, HALF_RB, BLK), w_src.reshape(RB_DEV, BLK)
    )
    scratch = [pltpu.VMEM((NONE + 8, BLK), f32)] * 2
    col = local_call(column_kernel, 4, NONE, scratch, "columns")(
        *shared, offsets.reshape(ROWS, BLK)
    )
    g_new = finish(col.reshape(NX * NC, HALF, BLK))
    return f_new.reshape(RB_DEV * BLK), g_new.reshape(TB_DEV * BLK)


def solution(mesh):
    fine = Mesh(mesh.devices.reshape(NX, NZ, NY, NC), ("x", "z", "y", "core"))
    src = ("x", "z", "y")
    placed = (
        P(None, src),
        P(src),
        P(None, src),
        P(src),
        P("core", src, None),
        P("core", src, None),
        P("core", src),
    )
    return jax.shard_map(
        on_device, mesh=fine, in_specs=placed, out_specs=(P(src), P(src)), check_vma=False
    )
```

time: 133 us -> 126 us (0.947)
  Pallas kernels: 124 us -> 120 us
  local copies, waits for them, and re-layouts: 7.58 us -> 4.8 us
    unnamed x10 -> x8, local copies, waits for them, and re-layouts: 6.08 us -> 3.3 us
    pallas_call x1, Pallas kernels: 17.6 us -> 15.5 us  [finish(): pl.pallas_call(finish_kernel, out_shape=jax.ShapeDtypeStruct((TB_DEV, BLK...]
    pallas_call x2, Pallas kernels: 20.5 us -> 22.5 us  [the longest x1 13.6 us: on_device(): partial = local_call(row_kernel, 3, ROWS, scratch, 'rows')(*shared)]
    pallas_call x1, Pallas kernels: 63.6 us -> 61.5 us  [gather(): pl.pallas_call(gather_kernel, out_shape=(pltpu.VMEM((LINES, DIM, X_LANES)...]
    pallas_call x1, Pallas kernels: 22.1 us -> 20.7 us  [exchange(): pl.pallas_call(exchange_kernel, out_shape=(jax.ShapeDtypeStruct((RB_DEV,...]
where the time goes in v4:
time: 126 us
  Pallas kernels  120 us (95%)
  local copies, waits for them, and re-layouts  4.8 us (4%)
    pallas_call x1, Pallas kernels, gather(): pl.pallas_call(gather_kernel, out_shape=(pltpu.VMEM((LINES, DIM, X_LANES)...  61.5 us
    pallas_call x1, Pallas kernels, exchange(): pl.pallas_call(exchange_kernel, out_shape=(jax.ShapeDtypeStruct((RB_DEV,...  20.7 us
    pallas_call x1, Pallas kernels, finish(): pl.pallas_call(finish_kernel, out_shape=jax.ShapeDtypeStruct((TB_DEV, BLK...  15.5 us
    pallas_call x1, Pallas kernels, on_device(): partial = local_call(row_kernel, 3, ROWS, scratch, 'rows')(*shared)  13.6 us
    pallas_call x1, Pallas kernels, on_device(): local_call(column_kernel, 4, NONE, scratch, 'columns')  8.92 us
    unnamed x8, local copies, waits for them, and re-layouts  3.3 us

profile of v4, /device:TPU:1, one launch (start us, length us, event | category | flops | bytes accessed | tf_op | source)
XLA Modules:
  0.0 125.8 jit_solution(1274596464647702655)
XLA Ops:
  0.6 0.7 reshape.27.w_ref
  1.4 0.8 reshape.25.g_ref
  2.1 0.0 copy-start
  2.1 0.7 copy-done
  2.8 0.0 copy-start.1
  2.8 0.7 copy-done.1
  3.5 0.0 copy-start.2
  3.5 0.7 copy-done.2
  4.2 61.5 %gather.1 = (bf16[32,64,2048]{2,1,0:T(8,128)(2,1)S(1)}, bf16[4,64,16384]{2,1,0:T(8,128)(2,1)S(1)}, f32[8,2,32,256]{3,2,1,0:T(8,128)S(1)}, s32[8,512]{1,0:T(8,128)S(1)}) custom-call(bf16[64,4096]{1,0:T(8,128)(2,1)} %x_ref.1, bf16[64,16384]{1,0:T(8,128)(2,1)} %y_ref.1, bf16[64,256]{1,0:T(8,128)(2,1)S(1)} %reshape.25.g_ref, s32[1,8,16]{2,1,0:T(8,128)S(1)} %bitcast.14, ...), custom_call_target="tpu_custom_call" | custom-call | tf_op jit(solution)/shard_map/gather/pallas_call | solution.py:493
  65.7 13.6 %rows.1 = f32[256,256]{1,0:T(8,128)S(1)} custom-call(s32[8,512]{1,0:T(8,128)S(1)} %get-tuple-element.8.items_ref, bf16[32,64,2048]{2,1,0:T(8,128)(2,1)S(1)} %get-tuple-element.9.x_ref, bf16[4,64,16384]{2,1,0:T(8,128)(2,1)S(1)} %get-tuple-element.10.y_ref, f32[8,2,32,256]{3,2,1,0:T(8,128)S(1)} %get-tuple-element.11.info_ref), custom_call_target="tpu_custom_call" | custom-call | tf_op jit(solution)/shard_map/rows/pallas_call | solution.py:696
  79.3 20.7 %exchange.1 = (f32[16,256]{1,0:T(8,128)S(1)}, f32[32,8,256]{2,1,0:T(8,128)S(1)}) custom-call(f32[32,8,256]{2,1,0:T(8,128)S(1)} %bitcast.10, f32[16,256]{1,0:T(8,128)S(1)} %reshape.27.w_ref), custom_call_target="tpu_custom_call" | custom-call | tf_op jit(solution)/shard_map/exchange/pallas_call | solution.py:608
  100.0 0.6 copy.9
  100.7 8.9 %columns.1 = f32[256,256]{1,0:T(8,128)S(1)} custom-call(s32[8,512]{1,0:T(8,128)S(1)} %get-tuple-element.8.items_ref, bf16[32,64,2048]{2,1,0:T(8,128)(2,1)S(1)} %get-tuple-element.9.x_ref, bf16[4,64,16384]{2,1,0:T(8,128)(2,1)S(1)} %get-tuple-element.10.y_ref, f32[8,2,32,256]{3,2,1,0:T(8,128)S(1)} %get-tuple-element.11.info_ref, f32[256,256]{1,0:T(8,128)S(1)} %bitcast.11), custom_call_target="tpu_custom_call" | custom-call | tf_op jit(solution)/shard_map/columns/pallas_call | solution.py:701
  109.6 15.5 %finish.1 = f32[64,256]{1,0:T(8,128)S(1)} custom-call(f32[8,32,256]{2,1,0:T(8,128)S(1)} %bitcast.9), custom_call_target="tpu_custom_call" | custom-call | tf_op jit(solution)/shard_map/finish/pallas_call | solution.py:671
  125.1 0.7 copy.10
Async XLA Ops:
  2.1 0.7 copy-start
  2.8 0.7 copy-start.1
  3.5 0.7 copy-start.2

commit v5 on v4

--- a/solution.py
+++ b/solution.py
@@ -196,13 +196,9 @@
 
 
 FIRST = ("Bl", "Bh", "A")
-PARTS = {"A": (0, 3, 1), "Bl": (3, 2, -1), "Bh": (5, 3, 1)}
+PARTS = {"A": (0, 768, 1), "Bl": (768, 512, -1), "Bh": (1280, 768, 1)}
 Y_CHUNKS = 4
 CHUNK = Y_LANES // Y_CHUNKS
-
-
-def anywhere():
-    return pl.BlockSpec(memory_space=pl.ANY)
 
 
 def place():
@@ -241,7 +237,7 @@
 
 
 def gather_plan():
-    took = {kind: part[1] * BLK for kind, part in PARTS.items()} | {"C": 4}
+    took = {kind: part[1] for kind, part in PARTS.items()} | {"C": 4}
     kinds = [f"Y{k}" for k in range(Y_CHUNKS)]
     took |= {kind: CHUNK for kind in kinds}
     first = [(kind, 0, 0) for kind in ["C", *FIRST, *kinds]]
@@ -264,9 +260,9 @@
 
 
 def gather_kernel(
-    x_ref, y_ref, g_ref, owner_ref, local_ref, live_ref,
+    x_ref, y_ref, g_hbm, owner_hbm, local_hbm, live_hbm,
     x_all, y_all, info_all, items_ref,
-    codes, y_own, info_sem, code_sem, code_send, own_sem, keep_sem, x_send, y_send, pair_sem, got,
+    codes, y_own, g_ref, owner_ref, local_ref, live_ref, small_sem, info_sem, code_sem, code_send, own_sem, keep_sem, x_send, y_send, pair_sem, got,
 ):
     x, z, y, c = place()
     turn = 1 - 2 * c
@@ -274,6 +270,14 @@
     first, order = gather_plan()
     index = {piece: k for k, piece in enumerate(order)}
 
+    small = [
+        pltpu.make_async_copy(there, here, small_sem.at[k])
+        for k, (there, here) in enumerate(
+            [(owner_hbm, owner_ref), (local_hbm, local_ref), (live_hbm, live_ref), (g_hbm, g_ref)]
+        )
+    ]
+    for copy in small:
+        copy.start()
     barrier = pltpu.get_barrier_semaphore()
     sibling = (x, z, y, 1 - c)
 
@@ -299,6 +303,8 @@
     exact = functools.partial(
         jnp.dot, preferred_element_type=jnp.float32, precision=lax.Precision.HIGHEST
     )
+    for copy in small:
+        copy.wait()
     slot_at = lax.broadcasted_iota(jnp.int32, (KH, RB_DEV), 0)
     listed = owner_ref[0] * HALF + local_ref[0]
     listed = jnp.where(slot_at < live_ref[...], listed, -1).astype(jnp.float32)
@@ -312,7 +318,7 @@
 
     def lanes_of(kind):
         if kind in PARTS:
-            return PARTS[kind][0] * BLK, PARTS[kind][1] * BLK
+            return PARTS[kind][:2]
         return int(kind[1:]) * CHUNK, CHUNK
 
     def slot(piece):
@@ -334,7 +340,7 @@
         begin, width = lanes_of(kind)
         if kind[0] == "Y":
             return y_ref.at[:, pl.ds(pl.multiple_of(y_mine + begin, BLK), width)]
-        return x_ref.at[:, pl.ds(pl.multiple_of(x_mine + begin, BLK), width)]
+        return x_ref.at[:, pl.ds(pl.multiple_of(x_mine + begin, 128), width)]
 
     def neighbour(axis, direction):
         step = turn * direction
@@ -368,8 +374,9 @@
             info[1, k : k + 1, :] = squares_of(y_own[:, k * BLK : (k + 1) * BLK])
 
     def do_info():
-        g_half = jnp.where(c == 0, g_ref[:HALF, :], g_ref[HALF:, :])
-        info[0] = OFFSET * g_half.astype(jnp.float32)
+        for k in range(HALF):
+            g_row = g_ref[pl.ds(pl.multiple_of((c * HALF + k) * BLK, BLK), BLK)]
+            info[0, k : k + 1, :] = OFFSET * g_row.astype(jnp.float32).reshape(1, BLK)
         for device in line_peers + [sibling]:
             pltpu.make_async_remote_copy(
                 src_ref=info,
@@ -498,11 +505,16 @@
             jax.ShapeDtypeStruct((NX * NC, 2, HALF, BLK), jnp.float32),
             jax.ShapeDtypeStruct((8, MOST), jnp.int32),
         ),
-        in_specs=[hbm, hbm, VMEM, VMEM, VMEM, VMEM],
+        in_specs=[hbm] * 6,
         out_specs=(VMEM, VMEM, VMEM, VMEM),
         scratch_shapes=[
             pltpu.VMEM((NC, LINES, 1, WIDE), jnp.int32),
             pltpu.VMEM((DIM, Y_LANES), jnp.bfloat16),
+            pltpu.VMEM(g_rows.shape, jnp.bfloat16),
+            pltpu.VMEM(owners.shape, jnp.int32),
+            pltpu.VMEM(locals_.shape, jnp.int32),
+            pltpu.VMEM(lives.shape, jnp.int32),
+            dma((4,)),
             dma((2,)),
             dma((2,)),
             dma,
@@ -538,23 +550,22 @@
     group = LINES
     me = z * NY + y
 
-    def peer(k):
-        other = lax.rem(me + k, group)
-        return other, (x, other // NY, other % NY, c)
+    def apart(size, step):
+        return min(step, size - step)
+
+    steps = [(dz, dy) for dz in range(NZ) for dy in range(NY) if dz or dy]
+    steps.sort(key=lambda by: -apart(NZ, by[0]) * NY - apart(NY, by[1]))
+    zs, ys = ([lax.rem(at + k, size) for k in range(size)] for at, size in ((z, NZ), (y, NY)))
+    peers = [(zs[dz] * NY + ys[dy], (x, zs[dz], ys[dy], c)) for dz, dy in steps]
 
     barrier = pltpu.get_barrier_semaphore()
-
-    def greet(k, carry):
-        pl.semaphore_signal(barrier, inc=1, device_id=peer(k)[1], device_id_type=MESH)
-        return carry
 
     sibling = (x, z, y, 1 - c)
     pl.semaphore_signal(barrier, inc=1, device_id=sibling, device_id_type=MESH)
-    lax.fori_loop(1, group, greet, 0)
+    for _, device in peers:
+        pl.semaphore_signal(barrier, inc=1, device_id=device, device_id_type=MESH)
     pl.semaphore_wait(barrier, group)
-
-    def send_part(k, carry):
-        other, device = peer(k)
+    for other, device in peers:
         pltpu.make_async_remote_copy(
             src_ref=part_ref.at[other],
             dst_ref=parts.at[me],
@@ -563,32 +574,31 @@
             device_id=device,
             device_id_type=MESH,
         ).start()
-        return carry
-
-    lax.fori_loop(1, group, send_part, 0)
     parts[me] = part_ref[me]
     others = parts.at[pl.ds(0, group - 1)]
     pltpu.make_async_copy(others, others, part_sem.at[1]).wait()
     f_half = potential(merged([parts[k] for k in range(group)]))
-    mine = pl.ds(pl.multiple_of(c * HALF_RB, HALF_RB), HALF_RB)
-    f_ref[mine, :] = f_half
-    bias_ref[me] = OFFSET * f_half + (EPSILON * OFFSET) * w_ref[mine, :]
-
-    def send_bias(k, carry):
+    for k in range(HALF_RB):
+        f_ref[pl.ds(pl.multiple_of((c * HALF_RB + k) * BLK, BLK), BLK)] = f_half[k]
+    mine = pl.ds(pl.multiple_of(c * X_LANES, X_LANES), X_LANES)
+    w_half = [
+        w_ref[pl.ds(pl.multiple_of((c * HALF_RB + k) * BLK, BLK), BLK)].reshape(1, BLK)
+        for k in range(HALF_RB)
+    ]
+    bias_ref[me] = OFFSET * f_half + (EPSILON * OFFSET) * jnp.concatenate(w_half, axis=0)
+
+    for _, device in peers:
         pltpu.make_async_remote_copy(
             src_ref=bias_ref.at[me],
             dst_ref=bias_ref.at[me],
             send_sem=bias_sem.at[0],
             recv_sem=bias_sem.at[1],
-            device_id=peer(k)[1],
+            device_id=device,
             device_id_type=MESH,
         ).start()
-        return carry
-
-    lax.fori_loop(1, group, send_bias, 0)
     over = pltpu.make_async_remote_copy(
-        src_ref=f_ref.at[mine, :],
-        dst_ref=f_ref.at[mine, :],
+        src_ref=f_ref.at[mine],
+        dst_ref=f_ref.at[mine],
         send_sem=f_sem.at[0],
         recv_sem=f_sem.at[1],
         device_id=sibling,
@@ -608,7 +618,7 @@
     return pl.pallas_call(
         exchange_kernel,
         out_shape=(
-            jax.ShapeDtypeStruct((RB_DEV, BLK), jnp.float32),
+            jax.ShapeDtypeStruct((RB_DEV * BLK,), jnp.float32),
             jax.ShapeDtypeStruct((group, HALF_RB, BLK), jnp.float32),
         ),
         in_specs=[VMEM, VMEM],
@@ -651,11 +661,12 @@
     others = parts.at[pl.ds(0, group - 1)]
     pltpu.make_async_copy(others, others, part_sem.at[1]).wait()
     g_half = potential(merged([parts[k] for k in range(group)]))
-    mine = pl.ds(pl.multiple_of(c * HALF, HALF), HALF)
-    g_ref[mine, :] = g_half
+    for k in range(HALF):
+        g_ref[pl.ds(pl.multiple_of((c * HALF + k) * BLK, BLK), BLK)] = g_half[k]
+    mine = pl.ds(pl.multiple_of(c * Y_LANES, Y_LANES), Y_LANES)
     over = pltpu.make_async_remote_copy(
-        src_ref=g_ref.at[mine, :],
-        dst_ref=g_ref.at[mine, :],
+        src_ref=g_ref.at[mine],
+        dst_ref=g_ref.at[mine],
         send_sem=g_sem.at[0],
         recv_sem=g_sem.at[1],
         device_id=sibling,
@@ -670,7 +681,7 @@
     dma = pltpu.SemaphoreType.DMA
     return pl.pallas_call(
         finish_kernel,
-        out_shape=jax.ShapeDtypeStruct((TB_DEV, BLK), jnp.float32),
+        out_shape=jax.ShapeDtypeStruct((TB_DEV * BLK,), jnp.float32),
         in_specs=[VMEM],
         out_specs=VMEM,
         scratch_shapes=[pltpu.VMEM((NX * NC, HALF, BLK), jnp.float32), dma((2,)), dma((2,))],
@@ -683,26 +694,28 @@
 
 def on_device(x_src, w_src, y_tgt, g_in, support_owner, support_local, live_count):
     f32 = jnp.float32
-    x_all, y_all, info, items = gather(
-        pltpu.with_memory_space_constraint(x_src, pltpu.HBM),
-        pltpu.with_memory_space_constraint(y_tgt, pltpu.HBM),
-        g_in.reshape(TB_DEV, BLK),
+    small = (
+        g_in,
         jnp.swapaxes(support_owner, 1, 2),
         jnp.swapaxes(support_local, 1, 2),
         live_count,
     )
+    given = [
+        pltpu.with_memory_space_constraint(array, pltpu.HBM) for array in (x_src, y_tgt, *small)
+    ]
+    x_all, y_all, info, items = gather(*given)
     shared = (items, x_all, y_all, info)
     scratch = [pltpu.VMEM((NX * NC + 1, ROWS, BLK), f32), pltpu.VMEM((NX * NC, HALF, BLK), f32)]
     partial = local_call(row_kernel, 3, ROWS, scratch, "rows")(*shared)
     f_new, offsets = exchange(
-        partial.reshape(LINES, HALF_RB, BLK), w_src.reshape(RB_DEV, BLK)
+        partial.reshape(LINES, HALF_RB, BLK), w_src
     )
     scratch = [pltpu.VMEM((NONE + 8, BLK), f32)] * 2
     col = local_call(column_kernel, 4, NONE, scratch, "columns")(
         *shared, offsets.reshape(ROWS, BLK)
     )
     g_new = finish(col.reshape(NX * NC, HALF, BLK))
-    return f_new.reshape(RB_DEV * BLK), g_new.reshape(TB_DEV * BLK)
+    return f_new, g_new
 
 
 def solution(mesh):

time: 126 us -> 121 us (0.960)
  local copies, waits for them, and re-layouts: 4.8 us -> 1.25 us
  Pallas kernels: 120 us -> 118 us
    pallas_call x1, Pallas kernels: 13.6 us -> 10.6 us  [on_device(): partial = local_call(row_kernel, 3, ROWS, scratch, 'rows')(*shared)]
    pallas_call x2, Pallas kernels: 36.3 us -> 39.1 us  [the longest x1 27.7 us: exchange(): pl.pallas_call(exchange_kernel, out_shape=(jax.ShapeDtypeStruct((RB_DEV *...]
    unnamed x8 -> x4, local copies, waits for them, and re-layouts: 3.3 us -> 1.25 us
    pallas_call x1, Pallas kernels: 8.92 us -> 6.96 us  [on_device(): local_call(column_kernel, 4, NONE, scratch, 'columns')]
    reshape x2 -> x0, local copies, waits for them, and re-layouts: 1.5 us -> none  [the longest x1 0.77 us: on_device(): g_in.reshape(TB_DEV, BLK)]
where the time goes in v5:
time: 121 us; the launch traced here: 120 us
  Pallas kernels  118 us (98%)
  local copies, waits for them, and re-layouts  1.25 us (1%)
    pallas_call x1, Pallas kernels, gather(): pl.pallas_call(gather_kernel, out_shape=(pltpu.VMEM((LINES, DIM, X_LANES)...  61.8 us
    pallas_call x1, Pallas kernels, exchange(): pl.pallas_call(exchange_kernel, out_shape=(jax.ShapeDtypeStruct((RB_DEV *...  27.7 us
    pallas_call x1, Pallas kernels, finish(): pl.pallas_call(finish_kernel, out_shape=jax.ShapeDtypeStruct((TB_DEV * BL...  11.5 us
    pallas_call x1, Pallas kernels, on_device(): partial = local_call(row_kernel, 3, ROWS, scratch, 'rows')(*shared)  10.6 us
    pallas_call x1, Pallas kernels, on_device(): local_call(column_kernel, 4, NONE, scratch, 'columns')  6.96 us

profile of v5, /device:TPU:1, one launch (start us, length us, event | category | flops | bytes accessed | tf_op | source)
XLA Modules:
  0.0 120.4 jit_solution(12434554064765041659)
XLA Ops:
  0.6 61.8 %gather.1 = (bf16[32,64,2048]{2,1,0:T(8,128)(2,1)S(1)}, bf16[4,64,16384]{2,1,0:T(8,128)(2,1)S(1)}, f32[8,2,32,256]{3,2,1,0:T(8,128)S(1)}, s32[8,512]{1,0:T(8,128)S(1)}) custom-call(bf16[64,4096]{1,0:T(8,128)(2,1)} %x_ref.1, bf16[64,16384]{1,0:T(8,128)(2,1)} %y_ref.1, bf16[16384]{0:T(1024)(128)(2,1)} %g_hbm.1, s32[1,8,16]{2,1,0:T(8,128)} %bitcast.8, ...), custom_call_target="tpu_custom_call" | custom-call | tf_op jit(solution)/shard_map/gather/pallas_call | solution.py:500
  62.4 0.0 copy-start
  62.4 10.6 %rows.1 = f32[256,256]{1,0:T(8,128)S(1)} custom-call(s32[8,512]{1,0:T(8,128)S(1)} %get-tuple-element.8.items_ref, bf16[32,64,2048]{2,1,0:T(8,128)(2,1)S(1)} %get-tuple-element.9.x_ref, bf16[4,64,16384]{2,1,0:T(8,128)(2,1)S(1)} %get-tuple-element.10.y_ref, f32[8,2,32,256]{3,2,1,0:T(8,128)S(1)} %get-tuple-element.11.info_ref), custom_call_target="tpu_custom_call" | custom-call | tf_op jit(solution)/shard_map/rows/pallas_call | solution.py:709
  73.0 0.0 copy-done
  73.0 27.7 %exchange.1 = (f32[4096]{0:T(1024)S(1)}, f32[32,8,256]{2,1,0:T(8,128)S(1)}) custom-call(f32[32,8,256]{2,1,0:T(8,128)S(1)} %bitcast.6, f32[4096]{0:T(1024)S(1)} %copy-done), custom_call_target="tpu_custom_call" | custom-call | tf_op jit(solution)/shard_map/exchange/pallas_call | solution.py:618
  100.7 7.0 %columns.1 = f32[256,256]{1,0:T(8,128)S(1)} custom-call(s32[8,512]{1,0:T(8,128)S(1)} %get-tuple-element.8.items_ref, bf16[32,64,2048]{2,1,0:T(8,128)(2,1)S(1)} %get-tuple-element.9.x_ref, bf16[4,64,16384]{2,1,0:T(8,128)(2,1)S(1)} %get-tuple-element.10.y_ref, f32[8,2,32,256]{3,2,1,0:T(8,128)S(1)} %get-tuple-element.11.info_ref, f32[256,256]{1,0:T(8,128)S(1)} %bitcast.7), custom_call_target="tpu_custom_call" | custom-call | tf_op jit(solution)/shard_map/columns/pallas_call | solution.py:714
  107.7 11.5 %finish.1 = f32[16384]{0:T(1024)S(1)} custom-call(f32[8,32,256]{2,1,0:T(8,128)S(1)} %bitcast.5), custom_call_target="tpu_custom_call" | custom-call | tf_op jit(solution)/shard_map/finish/pallas_call | solution.py:682
  119.1 0.6 copy.11
  119.7 0.6 copy.12
Async XLA Ops:
  62.4 10.6 %copy-start = (f32[4096]{0:T(1024)S(1)}, f32[4096]{0:T(1024)}, u32[]{:S(2)}) copy-start(f32[4096]{0:T(1024)} %w_ref.1) | copy-start | bytes 49156

commit v6 on v5

--- a/solution.py
+++ b/solution.py
@@ -35,7 +35,8 @@
 WIDE = RB_DEV * KH
 X_LANES = HALF_RB * BLK
 Y_LANES = HALF * BLK
-UNROLL = 16
+UNROLL = 32
+REST = 8
 SAFE = 100.0
 
 
@@ -83,13 +84,19 @@
 
 
 def for_pairs(items_ref, visit):
-    def step(group, carry):
-        for k in range(UNROLL):
-            code = items_ref[0, group * UNROLL + k]
-            visit(code // STRIDE, code % STRIDE)
-        return carry
-
-    lax.fori_loop(0, (items_ref[1, 0] + UNROLL - 1) // UNROLL, step, 0)
+    def groups(size, first, last):
+        def step(group, carry):
+            for k in range(size):
+                code = items_ref[0, first + group * size + k]
+                visit(code // STRIDE, code % STRIDE)
+            return carry
+
+        lax.fori_loop(0, (last - first + size - 1) // size, step, 0)
+
+    count = items_ref[1, 0]
+    whole = count // UNROLL * UNROLL
+    groups(UNROLL, 0, whole)
+    groups(REST, whole, count)
 
 
 def plain_mass(tile):

time: 121 us -> 118 us (0.975)
  Pallas kernels: 118 us -> 115 us
    pallas_call x1, Pallas kernels: 27.7 us -> 25.7 us  [exchange(): pl.pallas_call(exchange_kernel, out_shape=(jax.ShapeDtypeStruct((RB_DEV *...]
    pallas_call x1, Pallas kernels: 11.5 us -> 9.66 us  [finish(): pl.pallas_call(finish_kernel, out_shape=jax.ShapeDtypeStruct((TB_DEV * BL...]
where the time goes in v6:
time: 118 us; the launch traced here: 117 us
  Pallas kernels  115 us (97%)
  local copies, waits for them, and re-layouts  1.25 us (1%)
    pallas_call x1, Pallas kernels, gather(): pl.pallas_call(gather_kernel, out_shape=(pltpu.VMEM((LINES, DIM, X_LANES)...  61.8 us
    pallas_call x1, Pallas kernels, exchange(): pl.pallas_call(exchange_kernel, out_shape=(jax.ShapeDtypeStruct((RB_DEV *...  25.7 us
    pallas_call x1, Pallas kernels, on_device(): partial = local_call(row_kernel, 3, ROWS, scratch, 'rows')(*shared)  10.8 us
    pallas_call x1, Pallas kernels, finish(): pl.pallas_call(finish_kernel, out_shape=jax.ShapeDtypeStruct((TB_DEV * BL...  9.66 us
    pallas_call x1, Pallas kernels, on_device(): local_call(column_kernel, 4, NONE, scratch, 'columns')  7.07 us

profile of v6, /device:TPU:1, one launch (start us, length us, event | category | flops | bytes accessed | tf_op | source)
XLA Modules:
  0.0 116.9 jit_solution(9278529009692526703)
XLA Ops:
  0.6 61.8 %gather.1 = (bf16[32,64,2048]{2,1,0:T(8,128)(2,1)S(1)}, bf16[4,64,16384]{2,1,0:T(8,128)(2,1)S(1)}, f32[8,2,32,256]{3,2,1,0:T(8,128)S(1)}, s32[8,512]{1,0:T(8,128)S(1)}) custom-call(bf16[64,4096]{1,0:T(8,128)(2,1)} %x_ref.1, bf16[64,16384]{1,0:T(8,128)(2,1)} %y_ref.1, bf16[16384]{0:T(1024)(128)(2,1)} %g_hbm.1, s32[1,8,16]{2,1,0:T(8,128)} %bitcast.8, ...), custom_call_target="tpu_custom_call" | custom-call | tf_op jit(solution)/shard_map/gather/pallas_call | solution.py:507
  62.4 0.0 copy-start
  62.4 10.8 %rows.1 = f32[256,256]{1,0:T(8,128)S(1)} custom-call(s32[8,512]{1,0:T(8,128)S(1)} %get-tuple-element.8.items_ref, bf16[32,64,2048]{2,1,0:T(8,128)(2,1)S(1)} %get-tuple-element.9.x_ref, bf16[4,64,16384]{2,1,0:T(8,128)(2,1)S(1)} %get-tuple-element.10.y_ref, f32[8,2,32,256]{3,2,1,0:T(8,128)S(1)} %get-tuple-element.11.info_ref), custom_call_target="tpu_custom_call" | custom-call | tf_op jit(solution)/shard_map/rows/pallas_call | solution.py:716
  73.2 0.0 copy-done
  73.2 25.7 %exchange.1 = (f32[4096]{0:T(1024)S(1)}, f32[32,8,256]{2,1,0:T(8,128)S(1)}) custom-call(f32[32,8,256]{2,1,0:T(8,128)S(1)} %bitcast.6, f32[4096]{0:T(1024)S(1)} %copy-done), custom_call_target="tpu_custom_call" | custom-call | tf_op jit(solution)/shard_map/exchange/pallas_call | solution.py:625
  98.9 7.1 %columns.1 = f32[256,256]{1,0:T(8,128)S(1)} custom-call(s32[8,512]{1,0:T(8,128)S(1)} %get-tuple-element.8.items_ref, bf16[32,64,2048]{2,1,0:T(8,128)(2,1)S(1)} %get-tuple-element.9.x_ref, bf16[4,64,16384]{2,1,0:T(8,128)(2,1)S(1)} %get-tuple-element.10.y_ref, f32[8,2,32,256]{3,2,1,0:T(8,128)S(1)} %get-tuple-element.11.info_ref, f32[256,256]{1,0:T(8,128)S(1)} %bitcast.7), custom_call_target="tpu_custom_call" | custom-call | tf_op jit(solution)/shard_map/columns/pallas_call | solution.py:721
  106.0 9.7 %finish.1 = f32[16384]{0:T(1024)S(1)} custom-call(f32[8,32,256]{2,1,0:T(8,128)S(1)} %bitcast.5), custom_call_target="tpu_custom_call" | custom-call | tf_op jit(solution)/shard_map/finish/pallas_call | solution.py:689
  115.7 0.6 copy.11
  116.3 0.6 copy.12
Async XLA Ops:
  62.4 10.8 %copy-start = (f32[4096]{0:T(1024)S(1)}, f32[4096]{0:T(1024)}, u32[]{:S(2)}) copy-start(f32[4096]{0:T(1024)} %w_ref.1) | copy-start | bytes 49156
